TPU v7x, 512 devices: a whole 4x4x16 slice. The times are simulated.
512 devices in a mesh: seq: 16 (over z_lo, core), dp: 32 (over z_hi, x, y).
Axes of the slice: x: 4, y: 4, z: 16 (z_hi: 2, z_lo: 8; z = z_hi * 8 + z_lo), core: 2. Of those that a mesh axis runs over, the one named last changes fastest.
Arguments:
- frames: bfloat16 [32, 16, 512, 1152], P('dp', 'seq'), may hold values from -6 to 6
- shift_table: float32 [32, 1152], P('dp'), may hold values from -3 to 3
- scale_table: float32 [32, 1152], P('dp'), may hold values from -0.5 to 2
- grad_attended: bfloat16 [32, 16, 512, 576], P('dp', 'seq'), may hold values from -6 to 6
- w_qkv: bfloat16 [1152, 1728], P('seq'), may hold values from -0.1875 to 0.1875
Outputs:
- grad_frames: bfloat16 [32, 16, 512, 1152], P('dp', 'seq')
- grad_weight: bfloat16 [1152, 1728], P('seq')
All inputs are finite; a program needn't handle non-finite values.
Results may differ from a plain program's by a relative error of at most 0.035.
Values may be sent and summed in bfloat16 or wider, within the bound.
A program may use at most 64 MiB of HBM per device.

v0:
```python
import jax
import jax.numpy as jnp
from jax import lax
from jax.sharding import PartitionSpec as P

D = 1152
HD = 72


epsilon = 1e-06


def modulate(tokens, shift_row, scale_row):
    values = tokens.astype(jnp.float32)
    centre = jnp.mean(values, axis=-1, keepdims=True)
    centred = values - centre
    spread = jnp.mean(centred * centred, axis=-1, keepdims=True)
    return centred * lax.rsqrt(spread + epsilon) * (1.0 + scale_row) + shift_row


def attention_backward(projected, cotangent):
    frame_n, patch_n, columns = projected.shape
    inner = columns // 3
    head_n = inner // HD
    factor = HD ** (-0.5)
    query = projected[:, :, :inner].astype(jnp.float32).reshape(frame_n, patch_n, head_n, HD)
    key_rows = (
        projected[:, :, inner : 2 * inner].astype(jnp.float32).reshape(frame_n, patch_n, head_n, HD)
    )
    value_rows = (
        projected[:, :, 2 * inner :].astype(jnp.float32).reshape(frame_n, patch_n, head_n, HD)
    )
    grad_out = cotangent.astype(jnp.float32).reshape(frame_n, patch_n, head_n, HD)
    scores = jnp.einsum("fphd,gphd->phfg", query, key_rows) * factor
    highest = jnp.max(scores, axis=-1, keepdims=True)
    expo = jnp.exp(scores - highest)
    attend = expo / jnp.sum(expo, axis=-1, keepdims=True)
    attend_b = attend.astype(jnp.bfloat16).astype(jnp.float32)
    grad_value = jnp.einsum("phfg,fphd->gphd", attend_b, grad_out)
    dots = jnp.einsum("fphd,gphd->phfg", grad_out, value_rows)
    grad_scores = attend * (dots - jnp.sum(attend * dots, axis=-1, keepdims=True)) * factor
    grad_scores = grad_scores.astype(jnp.bfloat16).astype(jnp.float32)
    grad_query = jnp.einsum("phfg,gphd->fphd", grad_scores, key_rows)
    grad_key = jnp.einsum("phfg,fphd->gphd", grad_scores, query)
    joined = jnp.concatenate(
        [
            grad_query.reshape(frame_n, patch_n, inner),
            grad_key.reshape(frame_n, patch_n, inner),
            grad_value.reshape(frame_n, patch_n, inner),
        ],
        axis=-1,
    )
    return joined.astype(jnp.bfloat16)


def project(normed, full_weight):
    lead_a, lead_b, unused = normed.shape
    flat = jnp.dot(
        normed.reshape(-1, normed.shape[2]), full_weight, preferred_element_type=jnp.float32
    )
    return flat.astype(jnp.bfloat16).reshape(lead_a, lead_b, full_weight.shape[1])


def split_blocks(values, parts):
    lead, rows, width = values.shape
    return values.reshape(lead, parts, rows // parts, width)


def body(frames, shift_table, scale_table, grad_attended, w_qkv):
    tokens = frames[0]
    shift_row = shift_table[0]
    scale_row = scale_table[0]
    cotangent = grad_attended[0]
    columns = w_qkv.shape[1]
    seq_count = lax.axis_size("seq")
    normed = modulate(tokens, shift_row, scale_row).astype(jnp.bfloat16)
    full_weight = lax.all_gather(w_qkv, "seq", axis=0, tiled=True)
    cot_blocks = split_blocks(cotangent, seq_count)
    projected = project(normed, full_weight)
    pieces = (
        lax.all_to_all(
            split_blocks(projected, seq_count), "seq", split_axis=1, concat_axis=0, tiled=True
        ),
        lax.all_to_all(cot_blocks, "seq", split_axis=1, concat_axis=0, tiled=True),
    )
    frame_n, unused, count, width = pieces[0].shape
    result = attention_backward(
        pieces[0].reshape(frame_n, count, width),
        pieces[1].reshape(frame_n, count, pieces[1].shape[3]),
    )
    grad_patches = result.reshape(frame_n, 1, count, columns)
    grad_projected = lax.all_to_all(grad_patches, "seq", split_axis=0, concat_axis=1, tiled=True)
    grad_rows = grad_projected.reshape(-1, columns)
    token_rows = normed.reshape(-1, D)
    grad_normed = lax.dot_general(
        grad_rows,
        lax.all_gather(w_qkv, "seq", axis=0, tiled=True),
        (((1,), (1,)), ((), ())),
        preferred_element_type=jnp.float32,
    )
    unused, pull = jax.vjp(
        lambda inner_tokens: modulate(inner_tokens, shift_row, scale_row), tokens
    )
    grad_tokens = pull(grad_normed.reshape(tokens.shape))[0]
    frame_sum = lax.psum_scatter(
        lax.dot_general(
            token_rows, grad_rows, (((0,), (0,)), ((), ())), preferred_element_type=jnp.float32
        ).astype(jnp.bfloat16),
        "seq",
        scatter_dimension=0,
        tiled=True,
    ).astype(jnp.float32)
    video_sum = lax.psum(frame_sum, "dp")
    return (grad_tokens[None], video_sum.astype(jnp.bfloat16))


def solution(mesh):
    placed = (
        P("dp", "seq", None, None),
        P("dp", None),
        P("dp", None),
        P("dp", "seq", None, None),
        P("seq", None),
    )
    return jax.shard_map(
        body,
        mesh=mesh,
        in_specs=placed,
        out_specs=(P("dp", "seq", None, None), P("seq", None)),
        check_vma=False,
    )
```

profile of v0, /device:TPU:1, one launch (start us, length us, event | category | flops | bytes accessed | tf_op | source)
XLA Modules:
  0.0 1029.9 jit_solution(928301142258548355)
XLA Ops:
  7.9 2.1 copy.25
  10.1 14.0 %all-to-all-start.1 = ((bf16[1,16,32,576]{3,2,0,1:T(8,128)(2,1)}), bf16[1,16,32,576]{3,2,0,1:T(8,128)(2,1)S(1)}, u32[]{:S(2)}, u32[]{:S(2)}) async-start(bf16[1,16,32,576]{3,2,0,1:T(8,128)(2,1)} %bitcast.6), calls=%async_computation.1 | async-start | bytes 1310720 | tf_op jit(solution)/shard_map/all_to_all | solution.py:84
  24.9 97.4 %all-gather.2.cloned.1.call-done = bf16[1152,1728]{1,0:T(8,128)(2,1)} async-done(((bf16[72,1728]{1,0:T(8,128)(2,1)}), bf16[1152,1728]{1,0:T(8,128)(2,1)}) %all-gather.2.cloned.1.call-update) | async-done | bytes 3981328 | tf_op jit(solution)/shard_map/all_gather | solution.py:77
  122.3 6.1 convolution_convert_fusion.1
  128.4 3.8 copy.21
  133.1 10.5 %all-to-all-start = ((bf16[1,16,32,1728]{3,2,0,1:T(8,128)(2,1)}), bf16[1,16,32,1728]{3,2,0,1:T(8,128)(2,1)S(1)}, u32[]{:S(2)}, u32[]{:S(2)}) async-start(bf16[1,16,32,1728]{3,2,0,1:T(8,128)(2,1)} %bitcast.84), calls=%async_computation | async-start | bytes 3670016 | tf_op jit(solution)/shard_map/all_to_all | solution.py:81
  143.6 2.9 reshape.281
  146.6 69.0 %all-to-all-done = bf16[1,16,32,1728]{3,2,0,1:T(8,128)(2,1)S(1)} async-done(((bf16[1,16,32,1728]{3,2,0,1:T(8,128)(2,1)}), bf16[1,16,32,1728]{3,2,0,1:T(8,128)(2,1)S(1)}, u32[]{:S(2)}, u32[]{:S(2)}) %all-to-all-start) | async-done | bytes 1769504 | tf_op jit(solution)/shard_map/all_to_all | solution.py:81
  215.5 1.7 fusion.67
  217.3 3.0 reshape.279
  220.3 2.0 reshape.278
  222.3 2.4 reshape.280
  224.7 2.6 fusion.36
  227.3 4.8 fusion.68
  232.2 3.5 fusion.23
  235.6 6.2 fusion.22
  241.8 4.9 fusion.21
  246.8 1.5 copy.35
  248.2 1.7 concatenate.19
  249.9 1.6 copy.31
  251.5 1.7 concatenate.17
  253.4 1.7 concatenate.18
  255.1 2.8 concatenate.20
  257.9 100.3 %all_to_all.12 = bf16[16,1,32,1728]{3,2,1,0:T(8,128)(2,1)S(1)} all-to-all(bf16[16,1,32,1728]{3,2,1,0:T(8,128)(2,1)S(1)} %bitcast.85), channel_id=1, replica_groups=mesh['seq'=16,'dp'=32] {'seq'}, dimensions={0} | all-to-all | bytes 3538944 | tf_op jit(solution)/shard_map/all_to_all | solution.py:92
  358.2 1.3 copy-done.5
  359.5 4.5 convolution_convert_fusion
  364.0 1.4 copy-done.6
  365.4 4.9 fusion.9
  371.1 94.7 %reduce-scatter.2.cloned.1.call-done = bf16[72,1728]{1,0:T(8,128)(2,1)} async-done(((bf16[1152,1728]{1,0:T(8,128)(2,1)}), bf16[72,1728]{1,0:T(8,128)(2,1)}) %reduce-scatter.2.cloned.1.call-update) | async-done | bytes 248848 | tf_op jit(solution)/shard_map/reduce_scatter | solution.py:105
  465.8 1.2 fusion.24
  467.0 554.7 %all-reduce.2.cloned.1.call-done = bf16[72,1728]{1,0:T(8,128)(2,1)} async-done(((bf16[72,1728]{1,0:T(8,128)(2,1)}), bf16[72,1728]{1,0:T(8,128)(2,1)}) %all-reduce.2.cloned.1.call-update) | async-done | bytes 248848 | tf_op jit(solution)/shard_map/psum | solution.py:113
  1021.7 1.7 copy.69
  (35 shorter events, 3.5 us)
Async XLA Ops:
  7.2 17.0 %copy-start.9 = (f32[1,1152]{1,0:T(1,128)S(1)}, f32[1,1152]{1,0:T(1,128)}, u32[]{:S(2)}) copy-start(f32[1,1152]{1,0:T(1,128)} %param.6) | copy-start | bytes 13828
  7.2 17.0 %copy-start.8 = (f32[1,1152]{1,0:T(1,128)S(1)}, f32[1,1152]{1,0:T(1,128)}, u32[]{:S(2)}) copy-start(f32[1,1152]{1,0:T(1,128)} %param.7) | copy-start | bytes 13828
  7.2 17.0 %copy-start = (bf16[1,1,512,1152]{3,2,1,0:T(8,128)(2,1)S(1)}, bf16[1,1,512,1152]{3,2,1,0:T(8,128)(2,1)}, u32[]{:S(2)}) copy-start(bf16[1,1,512,1152]{3,2,1,0:T(8,128)(2,1)} %param.5) | copy-start | bytes 3538948
  7.2 115.1 %all-gather.2.cloned.1.call-start = ((), (), s32[]{:S(2)}) async-start(), calls=%async_computation.4 | async-start | bytes 4386816 | tf_op jit(solution)/shard_map/all_gather | solution.py:77
  10.1 122.1 %all-to-all-start.1 = ((bf16[1,16,32,576]{3,2,0,1:T(8,128)(2,1)}), bf16[1,16,32,576]{3,2,0,1:T(8,128)(2,1)S(1)}, u32[]{:S(2)}, u32[]{:S(2)}) async-start(bf16[1,16,32,576]{3,2,0,1:T(8,128)(2,1)} %bitcast.6), calls=%async_computation.1 | async-start | bytes 1310720 | tf_op jit(solution)/shard_map/all_to_all | solution.py:84
  132.2 0.9 copy-start.2
  133.1 82.5 %all-to-all-start = ((bf16[1,16,32,1728]{3,2,0,1:T(8,128)(2,1)}), bf16[1,16,32,1728]{3,2,0,1:T(8,128)(2,1)S(1)}, u32[]{:S(2)}, u32[]{:S(2)}) async-start(bf16[1,16,32,1728]{3,2,0,1:T(8,128)(2,1)} %bitcast.84), calls=%async_computation | async-start | bytes 3670016 | tf_op jit(solution)/shard_map/all_to_all | solution.py:81
  143.6 322.2 %reduce-scatter.2.cloned.1.call-start = ((), (), s32[]{:S(2)}) async-start(), calls=%async_computation.5 | async-start | bytes 4386816 | tf_op jit(solution)/shard_map/reduce_scatter | solution.py:105
  217.3 3.1 copy-start.3
  220.3 4.4 copy-start.1
  235.6 6.2 copy-start.4
  249.9 3.2 copy-start.7
  358.2 1.3 copy-start.5
  363.9 1.5 copy-start.6
  364.0 657.7 %all-reduce.2.cloned.1.call-start = ((), (), s32[]{:S(2)}) async-start(), calls=%async_computation.6 | async-start | bytes 516096 | tf_op jit(solution)/shard_map/psum | solution.py:113
Sparse Core Ops, SparseCore 0:
  10.1 112.1 all-gather.1
  364.1 101.6 reduce-scatter.1
  468.7 552.9 all-reduce.1
where the time goes:
time: 1050 us; the launch traced here: 1030 us
  waiting for transfers between devices  816 us (78%)
  blocking collectives  100 us (10%)
  matrix products  37.5 us (4%)
  local copies, waits for them, and re-layouts  34.4 us (3%)
  starting transfers between devices  24.7 us (2%)
  between operations  13.8 us (1%)
    psum x1, waiting for transfers between devices, body(): video_sum = lax.psum(frame_sum, 'dp')  555 us
    all_to_all x1, blocking collectives, body(): lax.all_to_all(grad_patches, 'seq', split_axis=0, concat_axis=1, tiled=True)  100 us
    all_gather x1, waiting for transfers between devices, body(): full_weight = lax.all_gather(w_qkv, 'seq', axis=0, tiled=True)  97.4 us
    reduce_scatter x1, waiting for transfers between devices, body(): lax.psum_scatter(lax.dot_general(token_rows, grad_rows, (((0,), (0,)), ((...  94.7 us
    all_to_all x1, waiting for transfers between devices, body(): lax.all_to_all(split_blocks(projected, seq_count), 'seq', split_axis=1, c...  69 us
  transfers between devices with their start and end apart: 5, of which 4 were waited for; matrix products, arithmetic and copies ran while one was open for 2% of the time, Pallas kernels for 0%

commit v1 on v0

v1 whole, which is shorter than its diff:
```python
import functools

import jax
import jax.numpy as jnp
from jax import lax
from jax.experimental import pallas as pl
from jax.experimental.pallas import tpu as pltpu
from jax.sharding import PartitionSpec as P

MESH = pl.DeviceIdType.MESH
F32 = jnp.float32
BF16 = jnp.bfloat16

D = 1152
HD = 72
INNER = 576
WIDE = 640
SEQ = 16
NZ = 8
NXY = 16
NQ = 16
ROWS = 72
PATCH = 512
OWN = 32
CH = 2
CP = 16
TOK = SEQ * CP
epsilon = 1e-06


def place():
    s, d = lax.axis_index("seq"), lax.axis_index("dp")
    return s, d, lax.div(s, 2), lax.rem(s, 2), lax.div(d, NXY), lax.rem(d, NXY)


def remote(src, dst, send, recv, seq, dp):
    return pltpu.make_async_remote_copy(
        src_ref=src,
        dst_ref=dst,
        send_sem=send,
        recv_sem=recv,
        device_id={"seq": seq, "dp": dp},
        device_id_type=MESH,
    )


def loop(start, stop, body):
    def step(i, carry):
        body(i)
        return carry

    lax.fori_loop(start, stop, step, 0)


def greet(seq, dp):
    pl.semaphore_signal(
        pltpu.get_barrier_semaphore(),
        inc=1,
        device_id={"seq": seq, "dp": dp},
        device_id_type=MESH,
    )


def gather_kernel(wp, w_out, g1, g2, g3, s1, r1, s2, r2, s3, r3, own_sem):
    s, d, z, c, hi, q = place()
    base = hi * NXY
    sibling = 2 * z + 1 - c
    loop(1, NZ, lambda i: greet(2 * lax.rem(z + i, NZ) + c, d))
    loop(1, NXY, lambda i: greet(s, base + lax.rem(q + i, NXY)))
    greet(sibling, d)
    pl.semaphore_wait(pltpu.get_barrier_semaphore(), NZ - 1 + NXY - 1 + 1)

    def along_z(i):
        return remote(wp.at[q], g1.at[z], s1.at[i - 1], r1.at[i - 1], 2 * lax.rem(z + i, NZ) + c, d)

    loop(1, NZ, lambda i: along_z(i).start())
    own = pltpu.make_async_copy(wp.at[q], g1.at[z], own_sem)
    own.start()
    own.wait()
    loop(1, NZ, lambda i: along_z(i).wait_recv())

    def over_plane(i):
        return remote(g1, g2.at[q], s2.at[i - 1], r2.at[i - 1], s, base + lax.rem(q + i, NXY))

    loop(1, NXY, lambda i: over_plane(i).start())
    own = pltpu.make_async_copy(g1, g2.at[q], own_sem)
    own.start()
    own.wait()

    def across(i):
        piece = lax.rem(q + NXY - i, NXY)
        return remote(g2.at[piece], g3.at[piece], s3.at[i], r3.at[i], sibling, d)

    across(0).start()

    def pass_on(i):
        over_plane(i).wait_recv()
        across(i).start()

    loop(1, NXY, pass_on)
    loop(0, NXY, lambda i: across(i).wait_recv())

    def assemble(t):
        piece, row = lax.div(t, NZ), lax.rem(t, NZ)
        part, tile = lax.div(piece, 5), lax.rem(piece, 5)
        here = g2[piece, row].astype(F32)
        there = g3[piece, row].astype(F32)
        both = jnp.concatenate([jnp.where(c == 0, here, there), jnp.where(c == 0, there, here)], axis=0)
        w_out[part, pl.ds(pl.multiple_of(row * 144, 16), 144), pl.ds(pl.multiple_of(tile * 128, 128), 128)] = (
            both.astype(BF16)
        )

    loop(0, 15 * NZ, assemble)
    loop(1, NZ, lambda i: along_z(i).wait_send())
    loop(1, NXY, lambda i: over_plane(i).wait_send())
    loop(0, NXY, lambda i: across(i).wait_send())


def gather(wp):
    return pl.pallas_call(
        gather_kernel,
        out_shape=jax.ShapeDtypeStruct((3, D, WIDE), BF16),
        in_specs=[pl.BlockSpec(memory_space=pltpu.VMEM)],
        out_specs=pl.BlockSpec(memory_space=pltpu.VMEM),
        scratch_shapes=[
            pltpu.VMEM((NZ, ROWS, 128), BF16),
            pltpu.VMEM((NQ, NZ, ROWS, 128), BF16),
            pltpu.VMEM((NQ, NZ, ROWS, 128), BF16),
            pltpu.SemaphoreType.DMA((NZ - 1,)),
            pltpu.SemaphoreType.DMA((NZ - 1,)),
            pltpu.SemaphoreType.DMA((NXY - 1,)),
            pltpu.SemaphoreType.DMA((NXY - 1,)),
            pltpu.SemaphoreType.DMA((NXY,)),
            pltpu.SemaphoreType.DMA((NXY,)),
            pltpu.SemaphoreType.DMA,
        ],
        compiler_params=pltpu.CompilerParams(
            collective_id=0, has_side_effects=True, vmem_limit_bytes=48 * 1024 * 1024
        ),
        name="gather_weight",
    )(wp)


def dot_last(a, b):
    return lax.dot_general(a, b, (((1,), (1,)), ((), ())), preferred_element_type=F32)


def dot_first(a, b):
    return lax.dot_general(a, b, (((0,), (0,)), ((), ())), preferred_element_type=F32)


def centred_of(tokens):
    values = tokens.astype(F32)
    centred = values - jnp.mean(values, axis=-1, keepdims=True)
    spread = jnp.mean(centred * centred, axis=-1, keepdims=True)
    return centred, lax.rsqrt(spread + epsilon)


def chunk_backward(ch, tokens, cots, shift, scale, w, away, proj, gproj, normed, cot, acc, gnorm, block):
    first = pl.multiple_of(ch * TOK, TOK)
    rows = pl.ds(first, TOK)
    gain = 1.0 + scale[...]

    def norm(f):
        centred, rate = centred_of(tokens[ch, f])
        normed[pl.ds(pl.multiple_of(first + f * CP, CP), CP), :] = (centred * rate * gain + shift[...]).astype(BF16)
        cot[pl.ds(pl.multiple_of(f * CP, CP), CP), :] = cots[ch, f]

    loop(0, SEQ, norm)

    def project(i):
        proj[i] = jnp.dot(normed[rows, :], w[i], preferred_element_type=F32).astype(BF16)
        acc[i] = jnp.zeros((TOK, WIDE), F32)

    loop(0, 3, project)
    factor = HD ** (-0.5)

    def heads(a):
        lanes = pl.ds(pl.multiple_of(a * 128, 128), 256)
        query, key, value, grad = proj[0, :, lanes], proj[1, :, lanes], proj[2, :, lanes], cot[:, lanes]
        lane = lax.broadcasted_iota(jnp.int32, (TOK, 256), 1)
        for t in range(2):
            low = 16 * a + HD * t
            mask = jnp.where((lane >= low) & (lane < low + HD), 1.0, 0.0).astype(BF16)
            query_h, key_h, grad_h = query * mask, key * mask, grad * mask
            scores = dot_last(query_h, key) * factor + block[...]
            expo = jnp.exp(scores - jnp.max(scores, axis=-1, keepdims=True))
            attend = expo / jnp.sum(expo, axis=-1, keepdims=True)
            acc[2, :, lanes] += dot_first(attend.astype(BF16), grad_h)
            dots = dot_last(grad_h, value)
            gscores = attend * (dots - jnp.sum(attend * dots, axis=-1, keepdims=True)) * factor
            gscores = gscores.astype(BF16)
            acc[0, :, lanes] += jnp.dot(gscores, key_h, preferred_element_type=F32)
            acc[1, :, lanes] += dot_first(gscores, query_h)

    loop(0, 4, heads)

    def rounded(i):
        gproj[i, rows, :] = acc[i].astype(BF16)

    loop(0, 3, rounded)

    def grad_normed(n):
        part = pl.ds(pl.multiple_of(n * 384, 128), 384)
        total = dot_last(gproj[0, rows, :], w[0, part, :])
        total += dot_last(gproj[1, rows, :], w[1, part, :])
        total += dot_last(gproj[2, rows, :], w[2, part, :])
        gnorm[:, part] = total

    loop(0, 3, grad_normed)

    def grad_tokens(f):
        centred, rate = centred_of(tokens[ch, f])
        unit = centred * rate
        grad = gnorm[pl.ds(pl.multiple_of(f * CP, CP), CP), :] * gain
        mean = jnp.mean(grad, axis=-1, keepdims=True)
        along = jnp.mean(grad * unit, axis=-1, keepdims=True)
        away[ch, f] = (rate * (grad - mean - unit * along)).astype(BF16)

    loop(0, SEQ, grad_tokens)


def weight_partial(normed, gproj, gw):
    def part(t):
        i, n = lax.div(t, 3), lax.rem(t, 3)
        cut = pl.ds(pl.multiple_of(n * 384, 128), 384)
        gw[i, cut, :] = dot_first(normed[:, cut], gproj[i])

    loop(0, 9, part)


def main_kernel(
    x, cot_in, shift, scale, w, out, gw,
    tokens, cots, away, proj, gproj, normed, cot, acc, gnorm, block,
    sx, rx, sc, rc, sb, rb, own_sems,
):
    s, d, z, c, hi, q = place()
    loop(1, SEQ, lambda i: greet(lax.rem(s + i, SEQ), d))
    pl.semaphore_wait(pltpu.get_barrier_semaphore(), SEQ - 1)

    def rows_of(j, ch):
        return pl.ds(pl.multiple_of(j * OWN + ch * CP, CP), CP)

    def send_x(ch, i):
        j = lax.rem(s + i, SEQ)
        return remote(x.at[rows_of(j, ch)], tokens.at[ch, s], sx.at[ch, i - 1], rx.at[ch, i - 1], j, d)

    def send_c(ch, i):
        j = lax.rem(s + i, SEQ)
        return remote(cot_in.at[rows_of(j, ch)], cots.at[ch, s], sc.at[ch, i - 1], rc.at[ch, i - 1], j, d)

    def send_back(ch, i):
        j = lax.rem(s + i, SEQ)
        return remote(away.at[ch, j], out.at[rows_of(s, ch)], sb.at[ch, i - 1], rb.at[ch, i - 1], j, d)

    for ch in range(CH):

        def both(i):
            send_x(ch, i).start()
            send_c(ch, i).start()

        loop(1, SEQ, both)
    keeps = []
    for ch in range(CH):
        keeps.append(pltpu.make_async_copy(x.at[rows_of(s, ch)], tokens.at[ch, s], own_sems.at[ch]))
        keeps.append(pltpu.make_async_copy(cot_in.at[rows_of(s, ch)], cots.at[ch, s], own_sems.at[CH + ch]))
    for keep in keeps:
        keep.start()
    row = lax.broadcasted_iota(jnp.int32, (TOK, TOK), 0)
    column = lax.broadcasted_iota(jnp.int32, (TOK, TOK), 1)
    block[...] = jnp.where(lax.rem(row, CP) == lax.rem(column, CP), 0.0, -1e30)
    for keep in keeps:
        keep.wait()

    def chunk(ch):
        def arrived(i):
            send_x(ch, i).wait_recv()
            send_c(ch, i).wait_recv()

        loop(1, SEQ, arrived)
        chunk_backward(ch, tokens, cots, shift, scale, w, away, proj, gproj, normed, cot, acc, gnorm, block)
        loop(1, SEQ, lambda i: send_back(ch, i).start())
        mine = pltpu.make_async_copy(away.at[ch, s], out.at[rows_of(s, ch)], own_sems.at[0])
        mine.start()
        mine.wait()

    loop(0, CH, chunk)
    weight_partial(normed, gproj, gw)

    def finish(ch):
        def ends(i):
            send_x(ch, i).wait_send()
            send_c(ch, i).wait_send()
            send_back(ch, i).wait()

        loop(1, SEQ, ends)

    loop(0, CH, finish)


def main(x, cot, shift, scale, w):
    vm = pl.BlockSpec(memory_space=pltpu.VMEM)
    dma = pltpu.SemaphoreType.DMA
    return pl.pallas_call(
        main_kernel,
        out_shape=(jax.ShapeDtypeStruct((PATCH, D), BF16), jax.ShapeDtypeStruct((3, D, WIDE), F32)),
        in_specs=[vm] * 5,
        out_specs=(vm, vm),
        scratch_shapes=[
            pltpu.VMEM((CH, SEQ, CP, D), BF16),
            pltpu.VMEM((CH, SEQ, CP, WIDE), BF16),
            pltpu.VMEM((CH, SEQ, CP, D), BF16),
            pltpu.VMEM((3, TOK, WIDE), BF16),
            pltpu.VMEM((3, CH * TOK, WIDE), BF16),
            pltpu.VMEM((CH * TOK, D), BF16),
            pltpu.VMEM((TOK, WIDE), BF16),
            pltpu.VMEM((3, TOK, WIDE), F32),
            pltpu.VMEM((TOK, D), F32),
            pltpu.VMEM((TOK, TOK), F32),
            dma((CH, SEQ - 1)),
            dma((CH, SEQ - 1)),
            dma((CH, SEQ - 1)),
            dma((CH, SEQ - 1)),
            dma((CH, SEQ - 1)),
            dma((CH, SEQ - 1)),
            dma((2 * CH,)),
        ],
        compiler_params=pltpu.CompilerParams(
            collective_id=1, has_side_effects=True, vmem_limit_bytes=56 * 1024 * 1024
        ),
        name="attention_backward",
    )(x, cot, shift, scale, w)


def reduce_kernel(gw, out, away, near, half, plane, line, column, s0, r0, s1, r1, s2, r2, s3, r3):
    s, d, z, c, hi, q = place()
    base = hi * NXY
    sibling = 2 * z + 1 - c
    greet(sibling, d)
    loop(1, NXY, lambda i: greet(s, base + lax.rem(q + i, NXY)))

    def on_line(i):
        t = lax.rem(hi * NZ + z + i, 2 * NZ)
        return 2 * lax.rem(t, NZ) + c, lax.div(t, NZ) * NXY + q

    loop(1, 2 * NZ, lambda i: greet(*on_line(i)))
    pl.semaphore_wait(pltpu.get_barrier_semaphore(), 1 + NXY - 1 + 2 * NZ - 1)

    def block(piece, row, core):
        part, tile = lax.div(piece, 5), lax.rem(piece, 5)
        first = pl.multiple_of(row * 144 + core * ROWS, 8)
        return gw[part, pl.ds(first, ROWS), pl.ds(pl.multiple_of(tile * 128, 128), 128)]

    def across(i):
        piece = lax.rem(q + i, NXY)
        return remote(away.at[piece], near.at[piece], s0.at[i], r0.at[i], sibling, d)

    def give(i):
        piece = lax.rem(q + i, NXY)
        source = jnp.minimum(piece, 14)

        def rows(row):
            away[piece, row] = block(source, row, 1 - c).astype(BF16)

        loop(0, NZ, rows)
        across(i).start()

    loop(0, NXY, give)

    def over_plane(i):
        peer = lax.rem(q + i, NXY)
        return remote(half.at[peer], plane.at[i - 1], s1.at[i - 1], r1.at[i - 1], s, base + peer)

    def add_core(i):
        piece = lax.rem(q + i, NXY)
        source = jnp.minimum(piece, 14)
        across(i).wait_recv()

        def rows(row):
            half[piece, row] = (block(source, row, c) + near[piece, row].astype(F32)).astype(BF16)

        loop(0, NZ, rows)

    def add_and_send(i):
        add_core(i)
        over_plane(i).start()

    loop(1, NXY, add_and_send)
    add_core(0)
    loop(1, NXY, lambda i: over_plane(i).wait_recv())

    def add_plane(row):
        total = half[q, row].astype(F32)
        for i in range(1, NXY):
            total += plane[i - 1, row].astype(F32)
        line[row] = total.astype(BF16)

    loop(0, NZ, add_plane)

    def along(i):
        t = lax.rem(hi * NZ + z + i, 2 * NZ)
        seq, dp = on_line(i)
        return remote(line.at[lax.rem(t, NZ)], column.at[i - 1], s2.at[i - 1], r2.at[i - 1], seq, dp)

    loop(1, 2 * NZ, lambda i: along(i).start())
    loop(1, 2 * NZ, lambda i: along(i).wait_recv())
    total = line[z].astype(F32)
    for i in range(1, 2 * NZ):
        total += column[i - 1].astype(F32)
    out[q] = total.astype(BF16)

    def spread(i):
        return remote(out.at[q], out.at[q], s3.at[i - 1], r3.at[i - 1], s, base + lax.rem(q + i, NXY))

    loop(1, NXY, lambda i: spread(i).start())
    loop(1, NXY, lambda i: spread(i).wait())
    loop(0, NXY, lambda i: across(i).wait_send())
    loop(1, NXY, lambda i: over_plane(i).wait_send())
    loop(1, 2 * NZ, lambda i: along(i).wait_send())


def reduce_weight(gw):
    dma = pltpu.SemaphoreType.DMA
    return pl.pallas_call(
        reduce_kernel,
        out_shape=jax.ShapeDtypeStruct((NQ, ROWS, 128), BF16),
        in_specs=[pl.BlockSpec(memory_space=pltpu.VMEM)],
        out_specs=pl.BlockSpec(memory_space=pltpu.VMEM),
        scratch_shapes=[
            pltpu.VMEM((NQ, NZ, ROWS, 128), BF16),
            pltpu.VMEM((NQ, NZ, ROWS, 128), BF16),
            pltpu.VMEM((NQ, NZ, ROWS, 128), BF16),
            pltpu.VMEM((NXY - 1, NZ, ROWS, 128), BF16),
            pltpu.VMEM((NZ, ROWS, 128), BF16),
            pltpu.VMEM((2 * NZ - 1, ROWS, 128), BF16),
            dma((NXY,)),
            dma((NXY,)),
            dma((NXY - 1,)),
            dma((NXY - 1,)),
            dma((2 * NZ - 1,)),
            dma((2 * NZ - 1,)),
            dma((NXY - 1,)),
            dma((NXY - 1,)),
        ],
        compiler_params=pltpu.CompilerParams(
            collective_id=2, has_side_effects=True, vmem_limit_bytes=48 * 1024 * 1024
        ),
        name="reduce_weight",
    )(gw)


def body(frames, shift_table, scale_table, grad_attended, w_qkv):
    wide = jnp.pad(w_qkv.reshape(ROWS, 3, INNER), ((0, 0), (0, 0), (0, WIDE - INNER)))
    wide = jnp.pad(wide.reshape(ROWS, 15, 128), ((0, 0), (0, 1), (0, 0)))
    full = gather(wide.transpose(1, 0, 2))
    cot = jnp.pad(grad_attended[0, 0], ((0, 0), (0, WIDE - INNER)))
    grad_tokens, gw = main(frames[0, 0], cot, shift_table, scale_table, full)
    total = reduce_weight(gw)
    total = total[:15].transpose(1, 0, 2).reshape(ROWS, 3, WIDE)[:, :, :INNER]
    return grad_tokens[None, None], total.reshape(ROWS, 3 * INNER)


def solution(mesh):
    placed = (
        P("dp", "seq", None, None),
        P("dp", None),
        P("dp", None),
        P("dp", "seq", None, None),
        P("seq", None),
    )
    return jax.shard_map(
        body,
        mesh=mesh,
        in_specs=placed,
        out_specs=(P("dp", "seq", None, None), P("seq", None)),
        check_vma=False,
    )
```

time: 1050 us -> 298 us (0.28); the launches traced: 1030 us -> 296 us
  waiting for transfers between devices: 816 us -> 0 us
  Pallas kernels: 0 us -> 287 us
  blocking collectives: 100 us -> 0 us
  matrix products: 37.5 us -> 0 us
  local copies, waits for them, and re-layouts: 34.4 us -> 7.72 us
  starting transfers between devices: 24.7 us -> 0 us
  between operations: 13.8 us -> 0.74 us
    psum x1 -> x0, waiting for transfers between devices: 555 us -> none  [body(): video_sum = lax.psum(frame_sum, 'dp')]
    pallas_call x0 -> x3, Pallas kernels: none -> 287 us  [the longest x1 143 us: main(): pl.pallas_call(main_kernel, out_shape=(jax.ShapeDtypeStruct((PATCH, D), B...]
    all_to_all x1 -> x0, blocking collectives: 100 us -> none  [body(): lax.all_to_all(grad_patches, 'seq', split_axis=0, concat_axis=1, tiled=True)]
    all_gather x1 -> x0, waiting for transfers between devices: 97.4 us -> none  [body(): full_weight = lax.all_gather(w_qkv, 'seq', axis=0, tiled=True)]
    reduce_scatter x1 -> x0, waiting for transfers between devices: 94.7 us -> none  [body(): lax.psum_scatter(lax.dot_general(token_rows, grad_rows, (((0,), (0,)), ((...]
    all_to_all x2 -> x0, waiting for transfers between devices: 69 us -> none  [the longest x1 69 us: body(): lax.all_to_all(split_blocks(projected, seq_count), 'seq', split_axis=1, c...]
    dot_general x7 -> x0, matrix products: 32.7 us -> none  [the longest x1 6.19 us: attention_backward(): grad_key = jnp.einsum('phfg,fphd->gphd', grad_scores, query)]
    all_to_all x2 -> x0, starting transfers between devices: 24.6 us -> none  [the longest x1 14 us: body(): lax.all_to_all(cot_blocks, 'seq', split_axis=1, concat_axis=0, tiled=True)]
  transfers between devices with their start and end apart: 5 -> 0, of which waited for: 4 -> 0; matrix products, arithmetic and copies ran while one was open for 2% -> 0% of each run, Pallas kernels for 0% -> 0%
where the time goes in v1:
time: 298 us; the launch traced here: 296 us
  Pallas kernels  287 us (96%)
  local copies, waits for them, and re-layouts  7.72 us (3%)
    pallas_call x1, Pallas kernels, main(): pl.pallas_call(main_kernel, out_shape=(jax.ShapeDtypeStruct((PATCH, D), B...  143 us
    pallas_call x1, Pallas kernels, reduce_weight(): pl.pallas_call(reduce_kernel, out_shape=jax.ShapeDtypeStruct((NQ, ROWS, 1...  89.6 us
    pallas_call x1, Pallas kernels, gather(): pl.pallas_call(gather_kernel, out_shape=jax.ShapeDtypeStruct((3, D, WIDE)...  54.4 us

profile of v1, /device:TPU:1, one launch (start us, length us, event | category | flops | bytes accessed | tf_op | source)
XLA Modules:
  0.0 295.8 jit_solution(3090280965066693337)
XLA Ops:
  0.6 1.1 reshape.16
  1.8 0.0 copy-start.2
  1.8 0.2 pad.13
  2.0 0.2 reshape.17
  2.2 0.1 copy.9
  2.3 0.5 copy-done.2
  2.8 0.3 copy.8
  3.1 0.9 pad.12.cot_in
  4.0 54.4 %gather_weight.1.w = bf16[3,1152,640]{2,1,0:T(8,128)(2,1)S(1)} custom-call(bf16[16,72,128]{2,1,0:T(8,128)(2,1)S(1)} %pad_bitcast_fusion.wp), custom_call_target="tpu_custom_call" | custom-call | tf_op jit(solution)/shard_map/gather_weight/pallas_call | solution.py:120
  58.4 0.0 copy-start
  58.5 2.1 copy-done
  60.5 143.3 %attention_backward.1 = (bf16[512,1152]{1,0:T(8,128)(2,1)}, f32[3,1152,640]{2,1,0:T(8,128)}) custom-call(bf16[512,1152]{1,0:T(8,128)(2,1)} %bitcast.11, bf16[512,640]{1,0:T(8,128)(2,1)} %pad.12.cot_in, f32[1,1152]{1,0:T(1,128)} %shift.1, f32[1,1152]{1,0:T(1,128)} %scale.1, bf16[3,1152,640]{2,1,0:T(8,128)(2,1)} %copy-done), custom_call_target="tpu_custom_call" | custom-call | tf_op jit(solution)/shard_map/attention_backward/pallas_call | solution.py:304
  203.9 89.6 %reduce_weight.1 = bf16[16,72,128]{2,1,0:T(8,128)(2,1)S(1)} custom-call(f32[3,1152,640]{2,1,0:T(8,128)} %get-tuple-element.5.gw), custom_call_target="tpu_custom_call" | custom-call | tf_op jit(solution)/shard_map/reduce_weight/pallas_call | solution.py:424
  293.5 0.0 copy-start.1
  293.5 0.1 copy.10
  293.6 0.2 reshape.18
  293.8 0.9 reshape.19
  294.7 0.1 copy-done.1
  294.8 1.0 copy.12
  (2 shorter events, 0.0 us)
Async XLA Ops:
  1.8 1.1 copy-start.2
  58.4 2.1 copy-start
  293.5 1.3 copy-start.1

commit v2 on v1

v2 whole, which is shorter than its diff:
```python
import jax
import jax.numpy as jnp
from jax import lax
from jax.experimental import pallas as pl
from jax.experimental.pallas import tpu as pltpu
from jax.sharding import PartitionSpec as P

MESH = pl.DeviceIdType.MESH
F32 = jnp.float32
BF16 = jnp.bfloat16

D = 1152
HD = 72
INNER = 576
WIDE = 640
SEQ = 16
NZ = 8
NXY = 16
NQ = 16
ROWS = 72
PATCH = 512
OWN = 32
CH = 2
CP = 16
TOK = SEQ * CP
epsilon = 1e-06


def place():
    s, d = lax.axis_index("seq"), lax.axis_index("dp")
    return s, d, lax.div(s, 2), lax.rem(s, 2), lax.div(d, NXY), lax.rem(d, NXY)


def remote(src, dst, send, recv, seq, dp):
    return pltpu.make_async_remote_copy(
        src_ref=src,
        dst_ref=dst,
        send_sem=send,
        recv_sem=recv,
        device_id={"seq": seq, "dp": dp},
        device_id_type=MESH,
    )


def loop(start, stop, body):
    def step(i, carry):
        body(i)
        return carry

    lax.fori_loop(start, stop, step, 0)


def greet(seq, dp):
    pl.semaphore_signal(
        pltpu.get_barrier_semaphore(),
        inc=1,
        device_id={"seq": seq, "dp": dp},
        device_id_type=MESH,
    )


def neighbours(me):
    return lax.rem(me + 1, 4), lax.rem(me + 3, 4), lax.rem(me + 2, 4)


def plane_device(h, stage, step, hi, x, y):
    along_x = (h == 0) == (stage == 0)
    me = x if along_x else y
    to = neighbours(me)[step]
    return hi * NXY + (to * 4 + y if along_x else x * 4 + to)


class Gather:
    def __init__(self, refs, spot):
        self.wp, self.w, self.g1, self.g2, self.g3, self.zs, self.zr, self.ps, self.pr, self.cs, self.cr, self.own = refs
        self.spot = spot

    def along_z(self, i):
        s, d, z, c, hi, q = self.spot
        return remote(
            self.wp.at[q], self.g1.at[z], self.zs.at[i - 1], self.zr.at[i - 1], 2 * lax.rem(z + i, NZ) + c, d
        )

    def plane(self, h, step, way):
        s, d, z, c, hi, q = self.spot
        x, y = lax.div(q, 4), lax.rem(q, 4)
        stage, passes = step // 2, step % 2
        low = 4 * h
        rows = pl.ds(low, 4)
        axis_x = (h == 0) == (stage == 0)
        other = neighbours(x if axis_x else y)[1 - way]
        if passes:
            rows = pl.ds(low + 2 * way, 2)
        if stage == 0:
            px, py = x, y
            if passes:
                px, py = (other, y) if axis_x else (x, other)
            piece = self.g2.at[px, py, rows]
        else:
            line = other if passes else (x if axis_x else y)
            piece = self.g2.at[line, :, rows] if axis_x else self.g2.at[:, line, rows]
        to = plane_device(h, stage, way, hi, x, y)
        return remote(piece, piece, self.ps.at[h, step, way], self.pr.at[h, step, way], s, to)

    def across(self, h, k):
        s, d, z, c, hi, q = self.spot
        x, y = lax.div(q, 4), lax.rem(q, 4)
        stage, which = k // 3, k % 3
        rows = pl.ds(4 * h, 4)
        axis_x = (h == 0) == (stage == 0)
        other = neighbours(x if axis_x else y)[which]

        def region(ref):
            if stage == 0:
                return ref.at[other, y, rows] if axis_x else ref.at[x, other, rows]
            return ref.at[other, :, rows] if axis_x else ref.at[:, other, rows]

        return remote(
            region(self.g2), region(self.g3), self.cs.at[h, k], self.cr.at[h, k], 2 * z + 1 - c, d
        )

    def own_across(self):
        s, d, z, c, hi, q = self.spot
        x, y = lax.div(q, 4), lax.rem(q, 4)
        return remote(self.g2.at[x, y], self.g3.at[x, y], self.cs.at[0, 6], self.cr.at[0, 6], 2 * z + 1 - c, d)

    def begin(self):
        loop(1, NZ, lambda i: self.along_z(i).start())

    def collect(self, between):
        s, d, z, c, hi, q = self.spot
        x, y = lax.div(q, 4), lax.rem(q, 4)
        own = pltpu.make_async_copy(self.wp.at[q], self.g1.at[z], self.own)
        own.start()
        own.wait()
        loop(1, NZ, lambda i: self.along_z(i).wait_recv())
        own = pltpu.make_async_copy(self.g1, self.g2.at[x, y], self.own)
        own.start()
        own.wait()
        for step in range(4):
            for h in range(2):
                if step:
                    for way in range(2):
                        self.plane(h, step - 1, way).wait_recv()
                for way in range(2):
                    self.plane(h, step, way).start()
                if step == 0 and h == 0:
                    self.own_across().start()
                if step % 2:
                    for k in range(2):
                        self.across(h, 3 * (step // 2) + k).start()
                elif step:
                    self.across(h, 2).start()
            between(step)
        for h in range(2):
            for way in range(2):
                self.plane(h, 3, way).wait_recv()
            self.across(h, 5).start()
        self.own_across().wait_recv()
        for h in range(2):
            for k in range(6):
                self.across(h, k).wait_recv()

        def assemble(t):
            piece, row = lax.div(t, NZ), lax.rem(t, NZ)
            part, tile = lax.div(piece, 5), lax.rem(piece, 5)
            px, py = lax.div(piece, 4), lax.rem(piece, 4)
            here = self.g2[px, py, row].astype(F32)
            there = self.g3[px, py, row].astype(F32)
            both = jnp.concatenate([jnp.where(c == 0, here, there), jnp.where(c == 0, there, here)], axis=0)
            lanes = pl.ds(pl.multiple_of(tile * 128, 128), 128)
            self.w[part, pl.ds(pl.multiple_of(row * 144, 16), 144), lanes] = both.astype(BF16)

        loop(0, 15 * NZ, assemble)

    def finish(self):
        loop(1, NZ, lambda i: self.along_z(i).wait_send())
        self.own_across().wait_send()
        for h in range(2):
            for step in range(4):
                for way in range(2):
                    self.plane(h, step, way).wait_send()
            for k in range(6):
                self.across(h, k).wait_send()


class Reduce:
    def __init__(self, refs, spot):
        (self.gw, self.out, self.away, self.near, self.half, self.a1, self.a2, self.b1, self.b2, self.column) = refs[:10]
        (self.cs, self.cr, self.ps, self.pr, self.zs, self.zr, self.ss, self.sr) = refs[10:]
        self.spot = spot

    def block(self, piece, row, core):
        part, tile = lax.div(piece, 5), lax.rem(piece, 5)
        first = pl.multiple_of(row * 144 + core * ROWS, 8)
        return self.gw[part, pl.ds(first, ROWS), pl.ds(pl.multiple_of(tile * 128, 128), 128)]

    def across(self, piece):
        s, d, z, c, hi, q = self.spot
        px, py = lax.div(piece, 4), lax.rem(piece, 4)
        return remote(
            self.away.at[px, py], self.near.at[px, py], self.cs.at[piece], self.cr.at[piece], 2 * z + 1 - c, d
        )

    def give(self, piece):
        c = self.spot[3]
        px, py = lax.div(piece, 4), lax.rem(piece, 4)

        def rows(row):
            self.away[px, py, row] = self.block(piece, row, 1 - c).astype(BF16)

        loop(0, NZ, rows)
        self.across(piece).start()

    def take(self, piece):
        c = self.spot[3]
        px, py = lax.div(piece, 4), lax.rem(piece, 4)
        self.across(piece).wait_recv()

        def rows(row):
            here = self.block(piece, row, c) + self.near[px, py, row].astype(F32)
            self.half[px, py, row] = here.astype(BF16)

        loop(0, NZ, rows)

    def clear(self):
        def rows(row):
            self.half[3, 3, row] = jnp.zeros((ROWS, 128), BF16)

        loop(0, NZ, rows)

    def cut(self, h, stage, where, low, count):
        q = self.spot[5]
        x, y = lax.div(q, 4), lax.rem(q, 4)
        rows = pl.ds(low, count)
        axis_x = (h == 0) == (stage == 0)
        if stage == 0:
            return self.half.at[where, :, rows] if axis_x else self.half.at[:, where, rows]
        return self.half.at[where, y, rows] if axis_x else self.half.at[x, where, rows]

    def plane(self, h, step, way):
        s, d, z, c, hi, q = self.spot
        x, y = lax.div(q, 4), lax.rem(q, 4)
        stage, second = step // 2, step % 2
        axis_x = (h == 0) == (stage == 0)
        near = neighbours(x if axis_x else y)
        if second:
            piece = self.cut(h, stage, near[way], 4 * h, 4)
        else:
            piece = self.cut(h, stage, near[2], 4 * h + 2 * way, 2)
        landing = ((self.a1, self.a2), (self.b1, self.b2))[stage][second].at[h, way]
        to = plane_device(h, stage, way, hi, x, y)
        return remote(piece, landing, self.ps.at[h, step, way], self.pr.at[h, step, way], s, to)

    def add(self, h, step):
        q = self.spot[5]
        x, y = lax.div(q, 4), lax.rem(q, 4)
        stage, second = step // 2, step % 2
        axis_x = (h == 0) == (stage == 0)
        me = x if axis_x else y
        near = neighbours(me)
        landing = ((self.a1, self.a2), (self.b1, self.b2))[stage][second]

        def spot_of(where, a, row):
            if stage == 0:
                return (where, a, row) if axis_x else (a, where, row)
            return (where, y, row) if axis_x else (x, where, row)

        def one(t):
            a, r = (lax.div(t, 4 if second else 2), lax.rem(t, 4 if second else 2))
            if second:
                at = spot_of(me, a, 4 * h + r)
                total = self.half[at].astype(F32)
                for way in range(2):
                    total += (landing[h, way, a, r] if stage == 0 else landing[h, way, r]).astype(F32)
                self.half[at] = total.astype(BF16)
            else:
                for way in range(2):
                    at = spot_of(near[way], a, 4 * h + 2 * way + r)
                    here = landing[h, way, a, r] if stage == 0 else landing[h, way, r]
                    self.half[at] = (self.half[at].astype(F32) + here.astype(F32)).astype(BF16)

        loop(0, (4 if stage == 0 else 1) * (4 if second else 2), one)

    def on_line(self, i):
        s, d, z, c, hi, q = self.spot
        t = lax.rem(hi * NZ + z + i, 2 * NZ)
        return 2 * lax.rem(t, NZ) + c, lax.div(t, NZ) * NXY + q, lax.rem(t, NZ)

    def along(self, i):
        q = self.spot[5]
        seq, dp, row = self.on_line(i)
        source = self.half.at[lax.div(q, 4), lax.rem(q, 4), row]
        return remote(source, self.column.at[i - 1], self.zs.at[i - 1], self.zr.at[i - 1], seq, dp)

    def spread(self, i):
        s, d, z, c, hi, q = self.spot
        to = hi * NXY + lax.rem(q + i, NXY)
        return remote(self.out.at[q], self.out.at[q], self.ss.at[i - 1], self.sr.at[i - 1], s, to)

    def sum_up(self):
        s, d, z, c, hi, q = self.spot
        loop(0, 15, self.take)
        for step in range(4):
            for h in range(2):
                if step:
                    for way in range(2):
                        self.plane(h, step - 1, way).wait_recv()
                    self.add(h, step - 1)
                for way in range(2):
                    self.plane(h, step, way).start()
        for h in range(2):
            for way in range(2):
                self.plane(h, 3, way).wait_recv()
            self.add(h, 3)
        loop(1, 2 * NZ, lambda i: self.along(i).start())
        loop(1, 2 * NZ, lambda i: self.along(i).wait_recv())
        total = self.half[lax.div(q, 4), lax.rem(q, 4), z].astype(F32)
        for i in range(1, 2 * NZ):
            total += self.column[i - 1].astype(F32)
        self.out[q] = total.astype(BF16)
        loop(1, NXY, lambda i: self.spread(i).start())
        loop(1, NXY, lambda i: self.spread(i).wait())

    def finish(self):
        loop(0, 15, lambda piece: self.across(piece).wait_send())
        for h in range(2):
            for step in range(4):
                for way in range(2):
                    self.plane(h, step, way).wait_send()
        loop(1, 2 * NZ, lambda i: self.along(i).wait_send())


def dot_last(a, b):
    return lax.dot_general(a, b, (((1,), (1,)), ((), ())), preferred_element_type=F32)


def dot_first(a, b):
    return lax.dot_general(a, b, (((0,), (0,)), ((), ())), preferred_element_type=F32)


def centred_of(tokens):
    values = tokens.astype(F32)
    centred = values - jnp.mean(values, axis=-1, keepdims=True)
    spread = jnp.mean(centred * centred, axis=-1, keepdims=True)
    return centred, lax.rsqrt(spread + epsilon)


def normalise(ch, f, tokens, cots, shift, scale, normed, cot):
    centred, rate = centred_of(tokens[ch, f])
    here = pl.ds(pl.multiple_of(ch * TOK + f * CP, CP), CP)
    normed[here, :] = (centred * rate * (1.0 + scale[...]) + shift[...]).astype(BF16)
    cot[pl.ds(pl.multiple_of(f * CP, CP), CP), :] = cots[ch, f]


def attention(ch, w, proj, gproj, normed, cot, acc, gnorm, block):
    rows = pl.ds(pl.multiple_of(ch * TOK, TOK), TOK)

    def project(i):
        proj[i] = jnp.dot(normed[rows, :], w[i], preferred_element_type=F32).astype(BF16)
        acc[i] = jnp.zeros((TOK, WIDE), F32)

    loop(0, 3, project)
    factor = HD ** (-0.5)

    def heads(a):
        lanes = pl.ds(pl.multiple_of(a * 128, 128), 256)
        query, key, value, grad = proj[0, :, lanes], proj[1, :, lanes], proj[2, :, lanes], cot[:, lanes]
        lane = lax.broadcasted_iota(jnp.int32, (TOK, 256), 1)
        for t in range(2):
            low = 16 * a + HD * t
            mask = jnp.where((lane >= low) & (lane < low + HD), 1.0, 0.0).astype(BF16)
            query_h, key_h, grad_h = query * mask, key * mask, grad * mask
            scores = dot_last(query_h, key) * factor + block[...]
            expo = jnp.exp(scores - jnp.max(scores, axis=-1, keepdims=True))
            attend = expo / jnp.sum(expo, axis=-1, keepdims=True)
            acc[2, :, lanes] += dot_first(attend.astype(BF16), grad_h)
            dots = dot_last(grad_h, value)
            gscores = attend * (dots - jnp.sum(attend * dots, axis=-1, keepdims=True)) * factor
            gscores = gscores.astype(BF16)
            acc[0, :, lanes] += jnp.dot(gscores, key_h, preferred_element_type=F32)
            acc[1, :, lanes] += dot_first(gscores, query_h)

    loop(0, 4, heads)

    def rounded(i):
        gproj[i, rows, :] = acc[i].astype(BF16)

    loop(0, 3, rounded)

    def grad_normed(n):
        part = pl.ds(pl.multiple_of(n * 384, 128), 384)
        total = dot_last(gproj[0, rows, :], w[0, part, :])
        total += dot_last(gproj[1, rows, :], w[1, part, :])
        total += dot_last(gproj[2, rows, :], w[2, part, :])
        gnorm[:, part] = total

    loop(0, 3, grad_normed)


def grad_tokens(ch, f, tokens, away, scale, gnorm):
    centred, rate = centred_of(tokens[ch, f])
    unit = centred * rate
    grad = gnorm[pl.ds(pl.multiple_of(f * CP, CP), CP), :] * (1.0 + scale[...])
    mean = jnp.mean(grad, axis=-1, keepdims=True)
    along = jnp.mean(grad * unit, axis=-1, keepdims=True)
    away[ch, f] = (rate * (grad - mean - unit * along)).astype(BF16)


def weight_partial(ch, i, normed, gproj, gw):
    rows = pl.ds(ch * TOK, TOK)

    def part(n):
        cut = pl.ds(pl.multiple_of(n * 384, 128), 384)
        term = dot_first(normed[rows, cut], gproj[i, rows, :])
        if ch == 0:
            gw[i, cut, :] = term
        else:
            gw[i, cut, :] += term

    loop(0, 3, part)


def kernel(
    x, cot_in, shift, scale, wp, out, gout,
    tokens, cots, away, proj, gproj, normed, cot, acc, gnorm, block, w, gw,
    g1, g2, g3, far, near, half, a1, a2, b1, b2, column,
    sx, rx, sc, rc, sb, rb, own_sems,
    gzs, gzr, gps, gpr, gcs, gcr, rcs, rcr, rps, rpr, rzs, rzr, rss, rsr,
):
    spot = place()
    s, d, z, c, hi, q = spot
    weight = Gather((wp, w, g1, g2, g3, gzs, gzr, gps, gpr, gcs, gcr, own_sems.at[4]), spot)
    total = Reduce(
        (gw, gout, far, near, half, a1, a2, b1, b2, column, rcs, rcr, rps, rpr, rzs, rzr, rss, rsr), spot
    )
    loop(1, SEQ, lambda i: greet(lax.rem(s + i, SEQ), d))
    loop(1, NXY, lambda i: greet(s, hi * NXY + lax.rem(q + i, NXY)))
    loop(0, NZ, lambda i: greet(2 * i + c, (1 - hi) * NXY + q))
    pl.semaphore_wait(pltpu.get_barrier_semaphore(), SEQ - 1 + NXY - 1 + NZ)

    def rows_of(j, ch):
        return pl.ds(pl.multiple_of(j * OWN + ch * CP, CP), CP)

    def send_x(ch, i):
        j = lax.rem(s + i, SEQ)
        return remote(x.at[rows_of(j, ch)], tokens.at[ch, s], sx.at[ch, i - 1], rx.at[ch, i - 1], j, d)

    def send_c(ch, i):
        j = lax.rem(s + i, SEQ)
        return remote(cot_in.at[rows_of(j, ch)], cots.at[ch, s], sc.at[ch, i - 1], rc.at[ch, i - 1], j, d)

    def send_back(ch, i):
        j = lax.rem(s + i, SEQ)
        return remote(away.at[ch, j], out.at[rows_of(s, ch)], sb.at[ch, i - 1], rb.at[ch, i - 1], j, d)

    def send_chunk(ch):
        def both(i):
            send_x(ch, i).start()
            send_c(ch, i).start()

        loop(1, SEQ, both)

    def between(step):
        if step == SECOND:
            send_chunk(1)

    weight.begin()
    send_chunk(0)
    keeps = []
    for ch in range(CH):
        keeps.append(pltpu.make_async_copy(x.at[rows_of(s, ch)], tokens.at[ch, s], own_sems.at[ch]))
        keeps.append(pltpu.make_async_copy(cot_in.at[rows_of(s, ch)], cots.at[ch, s], own_sems.at[CH + ch]))
    for keep in keeps:
        keep.start()
    weight.collect(between)
    row = lax.broadcasted_iota(jnp.int32, (TOK, TOK), 0)
    column_of = lax.broadcasted_iota(jnp.int32, (TOK, TOK), 1)
    block[...] = jnp.where(lax.rem(row, CP) == lax.rem(column_of, CP), 0.0, -1e30)
    for keep in keeps:
        keep.wait()
    total.clear()

    def chunk(ch):
        normalise(ch, s, tokens, cots, shift, scale, normed, cot)

        def arrived(i):
            send_x(ch, i).wait_recv()
            send_c(ch, i).wait_recv()
            normalise(ch, lax.rem(s + SEQ - i, SEQ), tokens, cots, shift, scale, normed, cot)

        loop(1, SEQ, arrived)
        attention(ch, w, proj, gproj, normed, cot, acc, gnorm, block)

        def leave(i):
            grad_tokens(ch, lax.rem(s + i, SEQ), tokens, away, scale, gnorm)
            send_back(ch, i).start()

        loop(1, SEQ, leave)
        grad_tokens(ch, s, tokens, away, scale, gnorm)
        mine = pltpu.make_async_copy(away.at[ch, s], out.at[rows_of(s, ch)], own_sems.at[0])
        mine.start()
        mine.wait()

    chunk(0)
    loop(0, 3, lambda i: weight_partial(0, i, normed, gproj, gw))
    chunk(1)

    def part(i):
        weight_partial(1, i, normed, gproj, gw)
        loop(0, 5, lambda t: total.give(5 * i + t))

    loop(0, 3, part)
    total.sum_up()
    total.finish()
    weight.finish()

    def finish(ch):
        def ends(i):
            send_x(ch, i).wait_send()
            send_c(ch, i).wait_send()
            send_back(ch, i).wait()

        loop(1, SEQ, ends)

    loop(0, CH, finish)


SECOND = 1


def fused(x, cot, shift, scale, wp):
    vm = pl.BlockSpec(memory_space=pltpu.VMEM)
    dma = pltpu.SemaphoreType.DMA
    return pl.pallas_call(
        kernel,
        out_shape=(jax.ShapeDtypeStruct((PATCH, D), BF16), jax.ShapeDtypeStruct((NQ, ROWS, 128), BF16)),
        in_specs=[vm] * 5,
        out_specs=(vm, vm),
        scratch_shapes=[
            pltpu.VMEM((CH, SEQ, CP, D), BF16),
            pltpu.VMEM((CH, SEQ, CP, WIDE), BF16),
            pltpu.VMEM((CH, SEQ, CP, D), BF16),
            pltpu.VMEM((3, TOK, WIDE), BF16),
            pltpu.VMEM((3, CH * TOK, WIDE), BF16),
            pltpu.VMEM((CH * TOK, D), BF16),
            pltpu.VMEM((TOK, WIDE), BF16),
            pltpu.VMEM((3, TOK, WIDE), F32),
            pltpu.VMEM((TOK, D), F32),
            pltpu.VMEM((TOK, TOK), F32),
            pltpu.VMEM((3, D, WIDE), BF16),
            pltpu.VMEM((3, D, WIDE), F32),
            pltpu.VMEM((NZ, ROWS, 128), BF16),
            pltpu.VMEM((4, 4, NZ, ROWS, 128), BF16),
            pltpu.VMEM((4, 4, NZ, ROWS, 128), BF16),
            pltpu.VMEM((4, 4, NZ, ROWS, 128), BF16),
            pltpu.VMEM((4, 4, NZ, ROWS, 128), BF16),
            pltpu.VMEM((4, 4, NZ, ROWS, 128), BF16),
            pltpu.VMEM((2, 2, 4, 2, ROWS, 128), BF16),
            pltpu.VMEM((2, 2, 4, 4, ROWS, 128), BF16),
            pltpu.VMEM((2, 2, 2, ROWS, 128), BF16),
            pltpu.VMEM((2, 2, 4, ROWS, 128), BF16),
            pltpu.VMEM((2 * NZ - 1, ROWS, 128), BF16),
        ]
        + [dma((CH, SEQ - 1))] * 6
        + [
            dma((5,)),
            dma((NZ - 1,)),
            dma((NZ - 1,)),
            dma((2, 4, 2)),
            dma((2, 4, 2)),
            dma((2, 7)),
            dma((2, 7)),
            dma((15,)),
            dma((15,)),
            dma((2, 4, 2)),
            dma((2, 4, 2)),
            dma((2 * NZ - 1,)),
            dma((2 * NZ - 1,)),
            dma((NXY - 1,)),
            dma((NXY - 1,)),
        ],
        compiler_params=pltpu.CompilerParams(
            collective_id=0, has_side_effects=True, vmem_limit_bytes=60 * 1024 * 1024
        ),
        name="temporal_backward",
    )(x, cot, shift, scale, wp)


def body(frames, shift_table, scale_table, grad_attended, w_qkv):
    wide = jnp.pad(w_qkv.reshape(ROWS, 3, INNER), ((0, 0), (0, 0), (0, WIDE - INNER)))
    wide = jnp.pad(wide.reshape(ROWS, 15, 128), ((0, 0), (0, 1), (0, 0)))
    cot = jnp.pad(grad_attended[0, 0], ((0, 0), (0, WIDE - INNER)))
    grad_tokens, total = fused(frames[0, 0], cot, shift_table, scale_table, wide.transpose(1, 0, 2))
    total = total[:15].transpose(1, 0, 2).reshape(ROWS, 3, WIDE)[:, :, :INNER]
    return grad_tokens[None, None], total.reshape(ROWS, 3 * INNER)


def solution(mesh):
    placed = (
        P("dp", "seq", None, None),
        P("dp", None),
        P("dp", None),
        P("dp", "seq", None, None),
        P("seq", None),
    )
    return jax.shard_map(
        body,
        mesh=mesh,
        in_specs=placed,
        out_specs=(P("dp", "seq", None, None), P("seq", None)),
        check_vma=False,
    )
```

time: 298 us -> 205 us (0.69)
  Pallas kernels: 287 us -> 195 us
    pallas_call x3 -> x1, Pallas kernels: 287 us -> 195 us  [fused(): pl.pallas_call(kernel, out_shape=(jax.ShapeDtypeStruct((PATCH, D), BF16),...]
where the time goes in v2:
time: 205 us; the launch traced here: 203 us
  Pallas kernels  195 us (95%)
  local copies, waits for them, and re-layouts  6.82 us (3%)
    pallas_call x1, Pallas kernels, fused(): pl.pallas_call(kernel, out_shape=(jax.ShapeDtypeStruct((PATCH, D), BF16),...  195 us

profile of v2, /device:TPU:1, one launch (start us, length us, event | category | flops | bytes accessed | tf_op | source)
XLA Modules:
  0.0 202.6 jit_solution(11574574876929305024)
XLA Ops:
  0.6 1.1 reshape.16
  1.8 0.0 copy-start.1
  1.8 0.2 pad.13
  2.0 0.2 reshape.17
  2.2 0.1 copy.9
  2.3 0.8 pad_bitcast_fusion.wp
  3.1 0.0 copy-done.1
  3.1 0.3 copy.8
  3.4 0.9 pad.12.cot_in
  4.3 195.1 %temporal_backward.1 = (bf16[512,1152]{1,0:T(8,128)(2,1)}, bf16[16,72,128]{2,1,0:T(8,128)(2,1)}) custom-call(bf16[512,1152]{1,0:T(8,128)(2,1)} %bitcast.11, bf16[512,640]{1,0:T(8,128)(2,1)} %pad.12.cot_in, f32[1,1152]{1,0:T(1,128)} %shift.1, f32[1,1152]{1,0:T(1,128)} %scale.1, bf16[16,72,128]{2,1,0:T(8,128)(2,1)} %pad_bitcast_fusion.wp), custom_call_target="tpu_custom_call" | custom-call | tf_op jit(solution)/shard_map/temporal_backward/pallas_call | solution.py:535
  199.3 0.0 copy-start
  199.4 1.1 slice_bitcast_fusion
  200.4 0.1 copy.10
  200.5 0.2 reshape.18
  200.6 0.9 reshape.19
  201.6 0.0 copy-done
  201.6 1.0 copy.12
Async XLA Ops:
  1.8 1.3 copy-start.1
  199.3 2.3 %copy-start = (bf16[512,1152]{1,0:T(8,128)(2,1)S(1)}, bf16[512,1152]{1,0:T(8,128)(2,1)}, u32[]{:S(2)}) copy-start(bf16[512,1152]{1,0:T(8,128)(2,1)} %get-tuple-element.4) | copy-start | bytes 3538948

commit v3 on v2

v3 whole, which is shorter than its diff:
```python
import jax
import jax.numpy as jnp
from jax import lax
from jax.experimental import pallas as pl
from jax.experimental.pallas import tpu as pltpu
from jax.sharding import PartitionSpec as P

MESH = pl.DeviceIdType.MESH
F32 = jnp.float32
BF16 = jnp.bfloat16

D = 1152
HD = 72
INNER = 576
WIDE = 640
SEQ = 16
NZ = 8
NXY = 16
NQ = 16
ROWS = 72
PATCH = 512
OWN = 32
CH = 4
CP = 8
GROUP = 4
TOK = SEQ * CP
epsilon = 1e-06


def place():
    s, d = lax.axis_index("seq"), lax.axis_index("dp")
    return s, d, lax.div(s, 2), lax.rem(s, 2), lax.div(d, NXY), lax.rem(d, NXY)


def remote(src, dst, send, recv, seq, dp):
    return pltpu.make_async_remote_copy(
        src_ref=src,
        dst_ref=dst,
        send_sem=send,
        recv_sem=recv,
        device_id={"seq": seq, "dp": dp},
        device_id_type=MESH,
    )


def loop(start, stop, body):
    def step(i, carry):
        body(i)
        return carry

    lax.fori_loop(start, stop, step, 0)


def greet(seq, dp):
    pl.semaphore_signal(
        pltpu.get_barrier_semaphore(),
        inc=1,
        device_id={"seq": seq, "dp": dp},
        device_id_type=MESH,
    )


def neighbours(me):
    return lax.rem(me + 1, 4), lax.rem(me + 3, 4), lax.rem(me + 2, 4)


def plane_device(h, stage, step, hi, x, y):
    along_x = (h == 0) == (stage == 0)
    me = x if along_x else y
    to = neighbours(me)[step]
    return hi * NXY + (to * 4 + y if along_x else x * 4 + to)


class Gather:
    def __init__(self, refs, spot):
        self.wp, self.w, self.g1, self.g2, self.g3, self.zs, self.zr, self.ps, self.pr, self.cs, self.cr, self.own = refs
        self.spot = spot

    def along_z(self, i):
        s, d, z, c, hi, q = self.spot
        four, at = lax.div(z, 4), lax.rem(z, 4)
        if isinstance(i, int) and i == 0:
            to = 2 * (4 * (1 - four) + at) + c
            return remote(self.wp.at[q], self.g1.at[four, at], self.zs.at[0], self.zr.at[0], to, d)
        to = 2 * (4 * four + lax.rem(at + i, 4)) + c
        return remote(self.g1.at[:, at], self.g1.at[:, at], self.zs.at[i], self.zr.at[i], to, d)

    def plane(self, h, step, way):
        s, d, z, c, hi, q = self.spot
        x, y = lax.div(q, 4), lax.rem(q, 4)
        stage, passes = step // 2, step % 2
        rows = pl.ds(2 * way, 2) if passes else slice(None)
        axis_x = (h == 0) == (stage == 0)
        other = neighbours(x if axis_x else y)[1 - way]
        if stage == 0:
            px, py = x, y
            if passes:
                px, py = (other, y) if axis_x else (x, other)
            piece = self.g2.at[px, py, h, rows]
        else:
            line = other if passes else (x if axis_x else y)
            piece = self.g2.at[line, :, h, rows] if axis_x else self.g2.at[:, line, h, rows]
        to = plane_device(h, stage, way, hi, x, y)
        return remote(piece, piece, self.ps.at[h, step, way], self.pr.at[h, step, way], s, to)

    def across(self, h, k):
        s, d, z, c, hi, q = self.spot
        x, y = lax.div(q, 4), lax.rem(q, 4)
        stage, which = k // 3, k % 3
        axis_x = (h == 0) == (stage == 0)
        other = neighbours(x if axis_x else y)[which]

        def region(ref):
            if stage == 0:
                return ref.at[other, y, h] if axis_x else ref.at[x, other, h]
            return ref.at[other, :, h] if axis_x else ref.at[:, other, h]

        return remote(
            region(self.g2), region(self.g3), self.cs.at[h, k], self.cr.at[h, k], 2 * z + 1 - c, d
        )

    def own_across(self):
        s, d, z, c, hi, q = self.spot
        x, y = lax.div(q, 4), lax.rem(q, 4)
        return remote(self.g2.at[x, y], self.g3.at[x, y], self.cs.at[0, 6], self.cr.at[0, 6], 2 * z + 1 - c, d)

    def begin(self):
        self.along_z(0).start()

    def collect(self, between):
        s, d, z, c, hi, q = self.spot
        x, y = lax.div(q, 4), lax.rem(q, 4)
        own = pltpu.make_async_copy(self.wp.at[q], self.g1.at[lax.div(z, 4), lax.rem(z, 4)], self.own)
        own.start()
        own.wait()
        self.along_z(0).wait_recv()
        loop(1, 4, lambda i: self.along_z(i).start())
        loop(1, 4, lambda i: self.along_z(i).wait_recv())
        own = pltpu.make_async_copy(self.g1, self.g2.at[x, y], self.own)
        own.start()
        own.wait()
        for step in range(4):
            for h in range(2):
                if step:
                    for way in range(2):
                        self.plane(h, step - 1, way).wait_recv()
                for way in range(2):
                    self.plane(h, step, way).start()
                if step == 0 and h == 0:
                    self.own_across().start()
                if step % 2:
                    for k in range(2):
                        self.across(h, 3 * (step // 2) + k).start()
                elif step:
                    self.across(h, 2).start()
            between(step)
        for h in range(2):
            for way in range(2):
                self.plane(h, 3, way).wait_recv()
            self.across(h, 5).start()
        self.own_across().wait_recv()
        for h in range(2):
            for k in range(6):
                self.across(h, k).wait_recv()

        def assemble(t):
            piece, row = lax.div(t, NZ), lax.rem(t, NZ)
            part, tile = lax.div(piece, 5), lax.rem(piece, 5)
            px, py = lax.div(piece, 4), lax.rem(piece, 4)
            here = self.g2[px, py, lax.div(row, 4), lax.rem(row, 4)].astype(F32)
            there = self.g3[px, py, lax.div(row, 4), lax.rem(row, 4)].astype(F32)
            both = jnp.concatenate([jnp.where(c == 0, here, there), jnp.where(c == 0, there, here)], axis=0)
            lanes = pl.ds(pl.multiple_of(tile * 128, 128), 128)
            self.w[part, pl.ds(pl.multiple_of(row * 144, 16), 144), lanes] = both.astype(BF16)

        loop(0, 15 * NZ, assemble)

    def finish(self):
        self.along_z(0).wait_send()
        loop(1, 4, lambda i: self.along_z(i).wait_send())
        self.own_across().wait_send()
        for h in range(2):
            for step in range(4):
                for way in range(2):
                    self.plane(h, step, way).wait_send()
            for k in range(6):
                self.across(h, k).wait_send()


class Reduce:
    def __init__(self, refs, spot):
        (self.gw, self.out, self.away, self.near, self.half, self.a1, self.a2, self.b1, self.b2, self.fours, self.column) = refs[:11]
        (self.cs, self.cr, self.ps, self.pr, self.zs, self.zr, self.ss, self.sr) = refs[11:]
        self.spot = spot

    def block(self, piece, row, core):
        part, tile = lax.div(piece, 5), lax.rem(piece, 5)
        first = pl.multiple_of(row * 144 + core * ROWS, 8)
        return self.gw[part, pl.ds(first, ROWS), pl.ds(pl.multiple_of(tile * 128, 128), 128)]

    def across(self, piece):
        s, d, z, c, hi, q = self.spot
        px, py = lax.div(piece, 4), lax.rem(piece, 4)
        return remote(
            self.away.at[px, py], self.near.at[px, py], self.cs.at[piece], self.cr.at[piece], 2 * z + 1 - c, d
        )

    def give(self, piece):
        c = self.spot[3]
        px, py = lax.div(piece, 4), lax.rem(piece, 4)

        def rows(row):
            self.away[px, py, row] = self.block(piece, row, 1 - c).astype(BF16)

        loop(0, NZ, rows)
        self.across(piece).start()

    def take(self, piece):
        c = self.spot[3]
        px, py = lax.div(piece, 4), lax.rem(piece, 4)
        self.across(piece).wait_recv()

        def rows(row):
            here = self.block(piece, row, c) + self.near[px, py, row].astype(F32)
            self.half[px, py, lax.div(row, 4), lax.rem(row, 4)] = here.astype(BF16)

        loop(0, NZ, rows)

    def clear(self):
        def rows(row):
            self.half[3, 3, lax.div(row, 4), lax.rem(row, 4)] = jnp.zeros((ROWS, 128), BF16)

        loop(0, NZ, rows)

    def cut(self, h, stage, where, low, count):
        q = self.spot[5]
        x, y = lax.div(q, 4), lax.rem(q, 4)
        rows = pl.ds(low, count)
        axis_x = (h == 0) == (stage == 0)
        if stage == 0:
            return self.half.at[where, :, h, rows] if axis_x else self.half.at[:, where, h, rows]
        return self.half.at[where, y, h, rows] if axis_x else self.half.at[x, where, h, rows]

    def plane(self, h, step, way):
        s, d, z, c, hi, q = self.spot
        x, y = lax.div(q, 4), lax.rem(q, 4)
        stage, second = step // 2, step % 2
        axis_x = (h == 0) == (stage == 0)
        near = neighbours(x if axis_x else y)
        if second:
            piece = self.cut(h, stage, near[way], 0, 4)
        else:
            piece = self.cut(h, stage, near[2], 2 * way, 2)
        landing = ((self.a1, self.a2), (self.b1, self.b2))[stage][second].at[h, way]
        to = plane_device(h, stage, way, hi, x, y)
        return remote(piece, landing, self.ps.at[h, step, way], self.pr.at[h, step, way], s, to)

    def add(self, h, step):
        q = self.spot[5]
        x, y = lax.div(q, 4), lax.rem(q, 4)
        stage, second = step // 2, step % 2
        axis_x = (h == 0) == (stage == 0)
        me = x if axis_x else y
        near = neighbours(me)
        landing = ((self.a1, self.a2), (self.b1, self.b2))[stage][second]

        def spot_of(where, a, row):
            if stage == 0:
                return (where, a, h, row) if axis_x else (a, where, h, row)
            return (where, y, h, row) if axis_x else (x, where, h, row)

        def one(t):
            a, r = (lax.div(t, 4 if second else 2), lax.rem(t, 4 if second else 2))
            if second:
                at = spot_of(me, a, r)
                total = self.half[at].astype(F32)
                for way in range(2):
                    total += (landing[h, way, a, r] if stage == 0 else landing[h, way, r]).astype(F32)
                self.half[at] = total.astype(BF16)
            else:
                for way in range(2):
                    at = spot_of(near[way], a, 2 * way + r)
                    here = landing[h, way, a, r] if stage == 0 else landing[h, way, r]
                    self.half[at] = (self.half[at].astype(F32) + here.astype(F32)).astype(BF16)

        loop(0, (4 if stage == 0 else 1) * (4 if second else 2), one)

    def in_four(self, i):
        s, d, z, c, hi, q = self.spot
        there = lax.rem(lax.rem(z, 4) + i, 4)
        source = self.half.at[lax.div(q, 4), lax.rem(q, 4), :, there]
        to = 2 * (4 * lax.div(z, 4) + there) + c
        return remote(source, self.fours.at[i - 1], self.zs.at[i - 1], self.zr.at[i - 1], to, d)

    def far_off(self, k):
        s, d, z, c, hi, q = self.spot
        four, at = lax.div(z, 4), lax.rem(z, 4)
        block = four if k == 2 else 1 - four
        source = self.half.at[lax.div(q, 4), lax.rem(q, 4), block, at]
        to = 2 * (4 * block + at) + c
        dp = d if k == 0 else (1 - hi) * NXY + q
        return remote(source, self.column.at[k], self.zs.at[3 + k], self.zr.at[3 + k], to, dp)

    def spread(self, i):
        s, d, z, c, hi, q = self.spot
        to = hi * NXY + lax.rem(q + i, NXY)
        return remote(self.out.at[q], self.out.at[q], self.ss.at[i - 1], self.sr.at[i - 1], s, to)

    def sum_up(self, beside):
        s, d, z, c, hi, q = self.spot
        loop(0, 15, self.take)
        for step in range(4):
            for h in range(2):
                if step:
                    for way in range(2):
                        self.plane(h, step - 1, way).wait_recv()
                    self.add(h, step - 1)
                for way in range(2):
                    self.plane(h, step, way).start()
        for h in range(2):
            for way in range(2):
                self.plane(h, 3, way).wait_recv()
            self.add(h, 3)
        px, py, four, at = lax.div(q, 4), lax.rem(q, 4), lax.div(z, 4), lax.rem(z, 4)
        loop(1, 4, lambda i: self.in_four(i).start())
        loop(1, 4, lambda i: self.in_four(i).wait_recv())
        for block in range(2):
            total = self.half[px, py, block, at].astype(F32)
            for i in range(3):
                total += self.fours[i, block].astype(F32)
            self.half[px, py, block, at] = total.astype(BF16)
        for k in range(3):
            self.far_off(k).start()
        beside()
        for k in range(3):
            self.far_off(k).wait_recv()
        total = self.half[px, py, four, at].astype(F32)
        for k in range(3):
            total += self.column[k].astype(F32)
        self.out[q] = total.astype(BF16)
        loop(1, NXY, lambda i: self.spread(i).start())
        loop(1, NXY, lambda i: self.spread(i).wait())

    def finish(self):
        loop(0, 15, lambda piece: self.across(piece).wait_send())
        for h in range(2):
            for step in range(4):
                for way in range(2):
                    self.plane(h, step, way).wait_send()
        loop(1, 4, lambda i: self.in_four(i).wait_send())
        for k in range(3):
            self.far_off(k).wait_send()


def dot_last(a, b):
    return lax.dot_general(a, b, (((1,), (1,)), ((), ())), preferred_element_type=F32)


def dot_first(a, b):
    return lax.dot_general(a, b, (((0,), (0,)), ((), ())), preferred_element_type=F32)


def centred_of(tokens):
    values = tokens.astype(F32)
    centred = values - jnp.mean(values, axis=-1, keepdims=True)
    spread = jnp.mean(centred * centred, axis=-1, keepdims=True)
    return centred, lax.rsqrt(spread + epsilon)


def chunk_rows(ch):
    return pl.ds(pl.multiple_of(ch * TOK, TOK), TOK)


def normalise(ch, tokens, cots, shift, scale, normed, cot):
    def group(g):
        centred, rate = centred_of(tokens[ch, pl.ds(g * GROUP, GROUP)].astype(F32).reshape(GROUP * CP, D))
        here = pl.ds(pl.multiple_of(ch * TOK + g * GROUP * CP, GROUP * CP), GROUP * CP)
        normed[here, :] = (centred * rate * (1.0 + scale[...]) + shift[...]).astype(BF16)
        here = pl.ds(pl.multiple_of(g * GROUP * CP, GROUP * CP), GROUP * CP)
        pair = cots[lax.div(ch, 2), pl.ds(g * GROUP, GROUP)].astype(F32).reshape(GROUP * CP, 2 * INNER)
        cot[here, :INNER] = jnp.where(lax.rem(ch, 2) == 0, pair[:, :INNER], pair[:, INNER:]).astype(BF16)

    loop(0, SEQ // GROUP, group)


def attention(ch, w, proj, gproj, normed, cot, block):
    rows = chunk_rows(ch)
    for i in range(3):
        proj[i] = jnp.dot(normed[rows, :], w[i], preferred_element_type=F32).astype(BF16)
    factor = HD ** (-0.5)
    lane = lax.broadcasted_iota(jnp.int32, (TOK, 256), 1)
    upper = [None] * 3
    for a in range(4):
        lanes = pl.ds(128 * a, 256)
        masks = []
        for t in range(2):
            low = 16 * a + HD * t
            masks.append(jnp.where((lane >= low) & (lane < low + HD), 1.0, 0.0).astype(BF16))

        def two(values):
            return jnp.concatenate([values * mask for mask in masks], axis=0)

        key, value = proj[1, :, lanes], proj[2, :, lanes]
        queries, keys, grads = two(proj[0, :, lanes]), two(key), two(cot[:, lanes])
        scores = dot_last(queries, key) * factor + block[...]
        expo = jnp.exp(scores - jnp.max(scores, axis=-1, keepdims=True))
        attend = expo / jnp.sum(expo, axis=-1, keepdims=True)
        dots = dot_last(grads, value)
        gscores = attend * (dots - jnp.sum(attend * dots, axis=-1, keepdims=True)) * factor
        gscores = gscores.astype(BF16)
        side = jnp.concatenate([gscores[:TOK], gscores[TOK:]], axis=1)
        found = (
            jnp.dot(side, keys, preferred_element_type=F32),
            dot_first(gscores, queries),
            dot_first(attend.astype(BF16), grads),
        )
        for i in range(3):
            lower = found[i][:, :128] if a == 0 else found[i][:, :128] + upper[i]
            gproj[i, rows, pl.ds(128 * a, 128)] = lower.astype(BF16)
            upper[i] = found[i][:, 128:]
    for i in range(3):
        gproj[i, rows, pl.ds(512, 128)] = upper[i].astype(BF16)


def grad_normed(ch, w, gproj, gnorm):
    rows = chunk_rows(ch)

    def part(n):
        cut = pl.ds(pl.multiple_of(n * 384, 128), 384)
        total = dot_last(gproj[0, rows, :], w[0, cut, :])
        total += dot_last(gproj[1, rows, :], w[1, cut, :])
        total += dot_last(gproj[2, rows, :], w[2, cut, :])
        gnorm[:, cut] = total

    loop(0, 3, part)


def grad_tokens(ch, g, tokens, away, scale, gnorm):
    frames = pl.ds(g * GROUP, GROUP)
    centred, rate = centred_of(tokens[ch, frames].astype(F32).reshape(GROUP * CP, D))
    unit = centred * rate
    grad = gnorm[pl.ds(pl.multiple_of(g * GROUP * CP, GROUP * CP), GROUP * CP), :] * (1.0 + scale[...])
    mean = jnp.mean(grad, axis=-1, keepdims=True)
    along = jnp.mean(grad * unit, axis=-1, keepdims=True)
    away[ch, frames] = (rate * (grad - mean - unit * along)).reshape(GROUP, CP, D).astype(BF16)


def weight_partial(first, count, i, normed, gproj, gw):
    rows = pl.ds(first * TOK, count * TOK)

    def part(n):
        cut = pl.ds(pl.multiple_of(n * 384, 128), 384)
        term = dot_first(normed[rows, cut], gproj[i, rows, :])
        if first == 0:
            gw[i, cut, :] = term
        else:
            gw[i, cut, :] += term

    loop(0, 3, part)


def narrow(parts):
    return jnp.concatenate([part[:, :INNER] for part in parts], axis=1)


def kernel(
    x, cot_in, shift, scale, w_in, out, gout,
    rows_in, turned, paired, wp, tiles, tokens, cots, away, proj, gproj, normed, cot, gnorm, block, w, gw,
    g1, g2, g3, far, near, half, a1, a2, b1, b2, fours, column,
    sx, rx, sc, rc, sb, rb, own_sems,
    gzs, gzr, gps, gpr, gcs, gcr, rcs, rcr, rps, rpr, rzs, rzr, rss, rsr,
):
    spot = place()
    s, d, z, c, hi, q = spot
    weight = Gather((wp, w, g1, g2, g3, gzs, gzr, gps, gpr, gcs, gcr, own_sems.at[0]), spot)
    total = Reduce(
        (gw, tiles, far, near, half, a1, a2, b1, b2, fours, column, rcs, rcr, rps, rpr, rzs, rzr, rss, rsr), spot
    )
    loop(1, SEQ, lambda i: greet(lax.rem(s + i, SEQ), d))
    loop(1, NXY, lambda i: greet(s, hi * NXY + lax.rem(q + i, NXY)))
    for at in (z, lax.rem(z + 4, NZ)):
        greet(2 * at + c, (1 - hi) * NXY + q)

    def group_of(j, ch):
        return j * CH + ch

    def send_x(ch, i):
        j = lax.rem(s + i, SEQ)
        return remote(x.at[group_of(j, ch)], tokens.at[ch, s], sx.at[ch, i - 1], rx.at[ch, i - 1], j, d)

    def send_c(pair, i):
        j = lax.rem(s + i, SEQ)
        return remote(paired.at[j, pair], cots.at[pair, s], sc.at[pair, i - 1], rc.at[pair, i - 1], j, d)

    def send_back(ch, i):
        j = lax.rem(s + i, SEQ)
        return remote(away.at[ch, j], out.at[group_of(s, ch)], sb.at[ch, i - 1], rb.at[ch, i - 1], j, d)

    def keep_back(ch):
        return pltpu.make_async_copy(away.at[ch, s], out.at[group_of(s, ch)], own_sems.at[1 + ch])

    def send_all(copy, k):
        loop(1, SEQ, lambda i: copy(k, i).start())

    def sent_all(copy, k):
        loop(1, SEQ, lambda i: copy(k, i).wait_send())

    def came_all(copy, k):
        loop(1, SEQ, lambda i: copy(k, i).wait_recv())

    def return_chunk(ch):
        loop(1, SEQ, lambda i: send_back(ch, i).start())
        keep_back(ch).start()

    load = pltpu.make_async_copy(w_in, rows_in, own_sems.at[0])
    turn = pltpu.make_async_copy(cot_in, turned, own_sems.at[1 + CH])
    load.start()
    turn.start()
    keeps = []
    for ch in range(CH):
        keeps.append(pltpu.make_async_copy(x.at[group_of(s, ch)], tokens.at[ch, s], own_sems.at[1 + ch]))
    for keep in keeps:
        keep.start()
    load.wait()
    pl.semaphore_wait(pltpu.get_barrier_semaphore(), SEQ - 1 + NXY - 1 + 2)

    gap = jnp.zeros((ROWS, WIDE - INNER), F32)
    for i in range(3):
        part = rows_in[:, pl.ds(i * INNER, INNER)].astype(F32)
        part = jnp.concatenate([part, gap], axis=1).astype(BF16)
        for t in range(5):
            wp[5 * i + t] = part[:, 128 * t : 128 * t + 128]
    wp[15] = jnp.zeros((ROWS, 128), BF16)
    weight.begin()
    send_all(send_x, 0)
    turn.wait()

    def pair_up(b):
        values = turned[:, pl.ds(pl.multiple_of(b * 128, 128), 128)].astype(F32).T
        values = values.reshape(4, 2, 2, CP, INNER)
        sides = jnp.concatenate([values[:, :, 0], values[:, :, 1]], axis=-1)
        paired[pl.ds(4 * b, 4)] = sides.astype(BF16)

    loop(0, 4, pair_up)
    send_all(send_c, 0)
    for pair in range(CH // 2):
        keeps.append(pltpu.make_async_copy(paired.at[s, pair], cots.at[pair, s], own_sems.at[1 + CH + pair]))
        keeps[-1].start()
    row = lax.broadcasted_iota(jnp.int32, (2 * TOK, TOK), 0)
    column_of = lax.broadcasted_iota(jnp.int32, (2 * TOK, TOK), 1)
    block[...] = jnp.where(lax.rem(row, CP) == lax.rem(column_of, CP), 0.0, -1e30)
    cot[:, pl.ds(512, 128)] = jnp.zeros((TOK, 128), BF16)
    total.clear()
    for keep in keeps:
        keep.wait()

    def between(step):
        if step == 0:
            send_all(send_x, 1)
        if step == 2:
            sent_all(send_x, 0)
            send_all(send_x, 2)
            send_all(send_c, 1)

    weight.collect(between)
    sent_all(send_x, 1)
    send_all(send_x, 3)

    def forward(ch):
        came_all(send_x, ch)

        @pl.when(lax.rem(ch, 2) == 0)
        def _():
            came_all(send_c, lax.div(ch, 2))

        normalise(ch, tokens, cots, shift, scale, normed, cot)
        attention(ch, w, proj, gproj, normed, cot, block)

    def backward(ch):
        grad_normed(ch, w, gproj, gnorm)
        loop(0, SEQ // GROUP, lambda g: grad_tokens(ch, g, tokens, away, scale, gnorm))

    def early(ch):
        forward(ch)
        backward(ch)

        @pl.when(ch == 1)
        def _():
            loop(0, 3, lambda i: weight_partial(0, 2, i, normed, gproj, gw))

    loop(0, 3, early)
    loop(0, 3, lambda i: weight_partial(2, 1, i, normed, gproj, gw))
    sent_all(send_x, 2)
    sent_all(send_x, 3)
    return_chunk(0)
    forward(3)

    def part(i):
        weight_partial(3, 1, i, normed, gproj, gw)
        loop(0, 5, lambda t: total.give(5 * i + t))

    loop(0, 3, part)
    return_chunk(1)
    backward(3)
    return_chunk(2)
    total.sum_up(lambda: return_chunk(3))
    gout[...] = narrow([jnp.concatenate([tiles[5 * i + t].astype(F32) for t in range(5)], axis=1) for i in range(3)]).astype(
        BF16
    )
    total.finish()
    weight.finish()
    for pair in range(CH // 2):
        sent_all(send_c, pair)

    def finish(ch):
        loop(1, SEQ, lambda i: send_back(ch, i).wait())
        keep_back(ch).wait()

    loop(0, CH, finish)


def fused(x, cot, shift, scale, w):
    vm, hbm = pl.BlockSpec(memory_space=pltpu.VMEM), pl.BlockSpec(memory_space=pl.ANY)
    dma = pltpu.SemaphoreType.DMA
    return pl.pallas_call(
        kernel,
        out_shape=(jax.ShapeDtypeStruct(x.shape, BF16), jax.ShapeDtypeStruct((ROWS, 3 * INNER), BF16)),
        in_specs=[hbm, hbm, vm, vm, hbm],
        out_specs=(vm, vm),
        scratch_shapes=[
            pltpu.VMEM((ROWS, 3 * INNER), BF16),
            pltpu.VMEM((INNER, PATCH), BF16),
            pltpu.VMEM((SEQ, CH // 2, CP, 2 * INNER), BF16),
            pltpu.VMEM((NQ, ROWS, 128), BF16),
            pltpu.VMEM((NQ, ROWS, 128), BF16),
            pltpu.VMEM((CH, SEQ, CP, D), BF16),
            pltpu.VMEM((CH // 2, SEQ, CP, 2 * INNER), BF16),
            pltpu.VMEM((CH, SEQ, CP, D), BF16),
            pltpu.VMEM((3, TOK, WIDE), BF16),
            pltpu.VMEM((3, CH * TOK, WIDE), BF16),
            pltpu.VMEM((CH * TOK, D), BF16),
            pltpu.VMEM((TOK, WIDE), BF16),
            pltpu.VMEM((TOK, D), F32),
            pltpu.VMEM((2 * TOK, TOK), F32),
            pltpu.VMEM((3, D, WIDE), BF16),
            pltpu.VMEM((3, D, WIDE), F32),
            pltpu.VMEM((2, 4, ROWS, 128), BF16),
            pltpu.VMEM((4, 4, 2, 4, ROWS, 128), BF16),
            pltpu.VMEM((4, 4, 2, 4, ROWS, 128), BF16),
            pltpu.VMEM((4, 4, NZ, ROWS, 128), BF16),
            pltpu.VMEM((4, 4, NZ, ROWS, 128), BF16),
            pltpu.VMEM((4, 4, 2, 4, ROWS, 128), BF16),
            pltpu.VMEM((2, 2, 4, 2, ROWS, 128), BF16),
            pltpu.VMEM((2, 2, 4, 4, ROWS, 128), BF16),
            pltpu.VMEM((2, 2, 2, ROWS, 128), BF16),
            pltpu.VMEM((2, 2, 4, ROWS, 128), BF16),
            pltpu.VMEM((3, 2, ROWS, 128), BF16),
            pltpu.VMEM((3, ROWS, 128), BF16),
        ]
        + [dma((CH, SEQ - 1))] * 2
        + [dma((CH // 2, SEQ - 1))] * 2
        + [dma((CH, SEQ - 1))] * 2
        + [
            dma((1 + 2 * CH,)),
            dma((4,)),
            dma((4,)),
            dma((2, 4, 2)),
            dma((2, 4, 2)),
            dma((2, 7)),
            dma((2, 7)),
            dma((15,)),
            dma((15,)),
            dma((2, 4, 2)),
            dma((2, 4, 2)),
            dma((6,)),
            dma((6,)),
            dma((NXY - 1,)),
            dma((NXY - 1,)),
        ],
        compiler_params=pltpu.CompilerParams(
            collective_id=0, has_side_effects=True, vmem_limit_bytes=60 * 1024 * 1024
        ),
        name="temporal_backward",
    )(x, cot, shift, scale, w)


def body(frames, shift_table, scale_table, grad_attended, w_qkv):
    x = frames.reshape(SEQ * CH, CP, D)
    cot = grad_attended[0, 0].T
    grad_tokens, grad_weight = fused(x, cot, shift_table, scale_table, w_qkv)
    return grad_tokens.reshape(frames.shape), grad_weight


def solution(mesh):
    placed = (
        P("dp", "seq", None, None),
        P("dp", None),
        P("dp", None),
        P("dp", "seq", None, None),
        P("seq", None),
    )
    return jax.shard_map(
        body,
        mesh=mesh,
        in_specs=placed,
        out_specs=(P("dp", "seq", None, None), P("seq", None)),
        check_vma=False,
    )
```

time: 205 us -> 192 us (0.937)
  Pallas kernels: 195 us -> 187 us
  local copies, waits for them, and re-layouts: 6.82 us -> 3.12 us
    pallas_call x1, Pallas kernels: 195 us -> 187 us  [fused(): pl.pallas_call(kernel, out_shape=(jax.ShapeDtypeStruct(x.shape, BF16), ja...]
    reshape x5 -> x0, local copies, waits for them, and re-layouts: 2.56 us -> none  [the longest x1 1.14 us: body(): w_qkv.reshape(ROWS, 3, INNER)]
where the time goes in v3:
time: 192 us; the launch traced here: 190 us
  Pallas kernels  187 us (97%)
  local copies, waits for them, and re-layouts  3.12 us (2%)
    pallas_call x1, Pallas kernels, fused(): pl.pallas_call(kernel, out_shape=(jax.ShapeDtypeStruct(x.shape, BF16), ja...  187 us

profile of v3, /device:TPU:1, one launch (start us, length us, event | category | flops | bytes accessed | tf_op | source)
XLA Modules:
  0.0 190.5 jit_solution(5119271864211223941)
XLA Ops:
  0.6 186.7 %temporal_backward.1 = (bf16[64,8,1152]{2,1,0:T(8,128)(2,1)}, bf16[72,1728]{1,0:T(8,128)(2,1)}) custom-call(bf16[64,8,1152]{2,1,0:T(8,128)(2,1)} %bitcast.5, bf16[576,512]{1,0:T(8,128)(2,1)} %bitcast.7, f32[1,1152]{1,0:T(1,128)} %shift.1, f32[1,1152]{1,0:T(1,128)} %scale.1, bf16[72,1728]{1,0:T(8,128)(2,1)} %w_in.1), custom_call_target="tpu_custom_call" | custom-call | tf_op jit(solution)/shard_map/temporal_backward/pallas_call | solution.py:625
  187.4 0.0 copy-start
  187.4 2.4 %copy.9 = bf16[1,1,512,1152]{3,2,1,0:T(8,128)(2,1)} copy(bf16[1,1,512,1152]{3,2,1,0:T(8,128)(2,1)} %bitcast.6) | data formatting | bytes 2359296
  189.8 0.0 copy-done
  189.8 0.7 copy.10
Async XLA Ops:
  187.4 2.4 %copy-start = (bf16[72,1728]{1,0:T(8,128)(2,1)S(1)}, bf16[72,1728]{1,0:T(8,128)(2,1)}, u32[]{:S(2)}) copy-start(bf16[72,1728]{1,0:T(8,128)(2,1)} %get-tuple-element.9) | copy-start | bytes 746500

commit v4 on v3

--- a/solution.py
+++ b/solution.py
@@ -133,8 +133,10 @@
         own = pltpu.make_async_copy(self.wp.at[q], self.g1.at[lax.div(z, 4), lax.rem(z, 4)], self.own)
         own.start()
         own.wait()
+        between(-2)
         self.along_z(0).wait_recv()
         loop(1, 4, lambda i: self.along_z(i).start())
+        between(-1)
         loop(1, 4, lambda i: self.along_z(i).wait_recv())
         own = pltpu.make_async_copy(self.g1, self.g2.at[x, y], self.own)
         own.start()
@@ -158,6 +160,7 @@
             for way in range(2):
                 self.plane(h, 3, way).wait_recv()
             self.across(h, 5).start()
+        between(4)
         self.own_across().wait_recv()
         for h in range(2):
             for k in range(6):
@@ -317,12 +320,14 @@
                     self.add(h, step - 1)
                 for way in range(2):
                     self.plane(h, step, way).start()
+            beside(step)
         for h in range(2):
             for way in range(2):
                 self.plane(h, 3, way).wait_recv()
             self.add(h, 3)
         px, py, four, at = lax.div(q, 4), lax.rem(q, 4), lax.div(z, 4), lax.rem(z, 4)
         loop(1, 4, lambda i: self.in_four(i).start())
+        beside(4)
         loop(1, 4, lambda i: self.in_four(i).wait_recv())
         for block in range(2):
             total = self.half[px, py, block, at].astype(F32)
@@ -331,7 +336,7 @@
             self.half[px, py, block, at] = total.astype(BF16)
         for k in range(3):
             self.far_off(k).start()
-        beside()
+        beside(5)
         for k in range(3):
             self.far_off(k).wait_recv()
         total = self.half[px, py, four, at].astype(F32)
@@ -339,6 +344,7 @@
             total += self.column[k].astype(F32)
         self.out[q] = total.astype(BF16)
         loop(1, NXY, lambda i: self.spread(i).start())
+        beside(6)
         loop(1, NXY, lambda i: self.spread(i).wait())
 
     def finish(self):
@@ -499,18 +505,22 @@
     def keep_back(ch):
         return pltpu.make_async_copy(away.at[ch, s], out.at[group_of(s, ch)], own_sems.at[1 + ch])
 
-    def send_all(copy, k):
-        loop(1, SEQ, lambda i: copy(k, i).start())
-
     def sent_all(copy, k):
         loop(1, SEQ, lambda i: copy(k, i).wait_send())
 
     def came_all(copy, k):
         loop(1, SEQ, lambda i: copy(k, i).wait_recv())
 
-    def return_chunk(ch):
-        loop(1, SEQ, lambda i: send_back(ch, i).start())
-        keep_back(ch).start()
+    order = ((send_x, 0), (send_c, 0), (send_x, 1), (send_x, 2), (send_c, 1), (send_x, 3))
+
+    def feed(first, last):
+        for k, (copy, which) in enumerate(order):
+            low, high = max(first - 15 * k, 0), min(last - 15 * k, 15)
+            if low < high:
+                loop(low + 1, high + 1, lambda i: copy(which, i).start())
+
+    def give_back(first, last):
+        loop(first, last, lambda n: send_back(lax.div(n, 15), lax.rem(n, 15) + 1).start())
 
     load = pltpu.make_async_copy(w_in, rows_in, own_sems.at[0])
     turn = pltpu.make_async_copy(cot_in, turned, own_sems.at[1 + CH])
@@ -532,8 +542,6 @@
             wp[5 * i + t] = part[:, 128 * t : 128 * t + 128]
     wp[15] = jnp.zeros((ROWS, 128), BF16)
     weight.begin()
-    send_all(send_x, 0)
-    turn.wait()
 
     def pair_up(b):
         values = turned[:, pl.ds(pl.multiple_of(b * 128, 128), 128)].astype(F32).T
@@ -541,30 +549,29 @@
         sides = jnp.concatenate([values[:, :, 0], values[:, :, 1]], axis=-1)
         paired[pl.ds(4 * b, 4)] = sides.astype(BF16)
 
-    loop(0, 4, pair_up)
-    send_all(send_c, 0)
-    for pair in range(CH // 2):
-        keeps.append(pltpu.make_async_copy(paired.at[s, pair], cots.at[pair, s], own_sems.at[1 + CH + pair]))
-        keeps[-1].start()
-    row = lax.broadcasted_iota(jnp.int32, (2 * TOK, TOK), 0)
-    column_of = lax.broadcasted_iota(jnp.int32, (2 * TOK, TOK), 1)
-    block[...] = jnp.where(lax.rem(row, CP) == lax.rem(column_of, CP), 0.0, -1e30)
-    cot[:, pl.ds(512, 128)] = jnp.zeros((TOK, 128), BF16)
-    total.clear()
-    for keep in keeps:
-        keep.wait()
-
     def between(step):
+        feed(FEEDS[step + 2], FEEDS[step + 3])
+        if step == -2:
+            turn.wait()
+            loop(0, 2, pair_up)
+        if step == -1:
+            loop(2, 4, pair_up)
+            for pair in range(CH // 2):
+                keeps.append(
+                    pltpu.make_async_copy(paired.at[s, pair], cots.at[pair, s], own_sems.at[1 + CH + pair])
+                )
+                keeps[-1].start()
         if step == 0:
-            send_all(send_x, 1)
-        if step == 2:
-            sent_all(send_x, 0)
-            send_all(send_x, 2)
-            send_all(send_c, 1)
+            row = lax.broadcasted_iota(jnp.int32, (2 * TOK, TOK), 0)
+            column_of = lax.broadcasted_iota(jnp.int32, (2 * TOK, TOK), 1)
+            block[...] = jnp.where(lax.rem(row, CP) == lax.rem(column_of, CP), 0.0, -1e30)
+            cot[:, pl.ds(512, 128)] = jnp.zeros((TOK, 128), BF16)
+            total.clear()
+            for keep in keeps:
+                keep.wait()
 
     weight.collect(between)
-    sent_all(send_x, 1)
-    send_all(send_x, 3)
+    feed(FEEDS[7], 90)
 
     def forward(ch):
         came_all(send_x, ch)
@@ -583,6 +590,7 @@
     def early(ch):
         forward(ch)
         backward(ch)
+        keep_back(ch).start()
 
         @pl.when(ch == 1)
         def _():
@@ -590,9 +598,8 @@
 
     loop(0, 3, early)
     loop(0, 3, lambda i: weight_partial(2, 1, i, normed, gproj, gw))
-    sent_all(send_x, 2)
     sent_all(send_x, 3)
-    return_chunk(0)
+    give_back(0, RETURNS[0])
     forward(3)
 
     def part(i):
@@ -600,10 +607,15 @@
         loop(0, 5, lambda t: total.give(5 * i + t))
 
     loop(0, 3, part)
-    return_chunk(1)
-    backward(3)
-    return_chunk(2)
-    total.sum_up(lambda: return_chunk(3))
+    give_back(RETURNS[0], RETURNS[1])
+
+    def beside(step):
+        if step == 0:
+            backward(3)
+            keep_back(3).start()
+        give_back(RETURNS[step + 1], RETURNS[step + 2])
+
+    total.sum_up(beside)
     gout[...] = narrow([jnp.concatenate([tiles[5 * i + t].astype(F32) for t in range(5)], axis=1) for i in range(3)]).astype(
         BF16
     )
@@ -611,12 +623,18 @@
     weight.finish()
     for pair in range(CH // 2):
         sent_all(send_c, pair)
+    for ch in range(3):
+        sent_all(send_x, ch)
 
     def finish(ch):
         loop(1, SEQ, lambda i: send_back(ch, i).wait())
         keep_back(ch).wait()
 
     loop(0, CH, finish)
+
+
+FEEDS = (0, 6, 11, 16, 20, 30, 36, 40)
+RETURNS = (10, 20, 25, 34, 39, 43, 47, 51, 60)
 
 
 def fused(x, cot, shift, scale, w):

time: 192 us -> 175 us (0.911)
  Pallas kernels: 187 us -> 171 us
    pallas_call x1, Pallas kernels: 187 us -> 171 us  [fused(): pl.pallas_call(kernel, out_shape=(jax.ShapeDtypeStruct(x.shape, BF16), ja...]
where the time goes in v4:
time: 175 us
  Pallas kernels  171 us (98%)
  local copies, waits for them, and re-layouts  3.12 us (2%)
    pallas_call x1, Pallas kernels, fused(): pl.pallas_call(kernel, out_shape=(jax.ShapeDtypeStruct(x.shape, BF16), ja...  171 us

profile of v4, /device:TPU:1, one launch (start us, length us, event | category | flops | bytes accessed | tf_op | source)
XLA Modules:
  0.0 175.1 jit_solution(14703936935818133875)
XLA Ops:
  0.6 171.4 %temporal_backward.1 = (bf16[64,8,1152]{2,1,0:T(8,128)(2,1)}, bf16[72,1728]{1,0:T(8,128)(2,1)}) custom-call(bf16[64,8,1152]{2,1,0:T(8,128)(2,1)} %bitcast.5, bf16[576,512]{1,0:T(8,128)(2,1)} %bitcast.7, f32[1,1152]{1,0:T(1,128)} %shift.1, f32[1,1152]{1,0:T(1,128)} %scale.1, bf16[72,1728]{1,0:T(8,128)(2,1)} %w_in.1), custom_call_target="tpu_custom_call" | custom-call | tf_op jit(solution)/shard_map/temporal_backward/pallas_call | solution.py:643
  172.0 0.0 copy-start
  172.0 2.4 %copy.9 = bf16[1,1,512,1152]{3,2,1,0:T(8,128)(2,1)} copy(bf16[1,1,512,1152]{3,2,1,0:T(8,128)(2,1)} %bitcast.6) | data formatting | bytes 2359296
  174.4 0.0 copy-done
  174.4 0.7 copy.10
Async XLA Ops:
  172.0 2.4 %copy-start = (bf16[72,1728]{1,0:T(8,128)(2,1)S(1)}, bf16[72,1728]{1,0:T(8,128)(2,1)}, u32[]{:S(2)}) copy-start(bf16[72,1728]{1,0:T(8,128)(2,1)} %get-tuple-element.9) | copy-start | bytes 746500

commit v5 on v4

--- a/solution.py
+++ b/solution.py
@@ -201,92 +201,97 @@
         first = pl.multiple_of(row * 144 + core * ROWS, 8)
         return self.gw[part, pl.ds(first, ROWS), pl.ds(pl.multiple_of(tile * 128, 128), 128)]
 
-    def across(self, piece):
-        s, d, z, c, hi, q = self.spot
-        px, py = lax.div(piece, 4), lax.rem(piece, 4)
-        return remote(
-            self.away.at[px, py], self.near.at[px, py], self.cs.at[piece], self.cr.at[piece], 2 * z + 1 - c, d
-        )
-
-    def give(self, piece):
+    def lines(self, h, stage=0):
+        q = self.spot[5]
+        axis_x = (h == 0) == (stage == 0)
+        me = lax.div(q, 4) if axis_x else lax.rem(q, 4)
+        plus, minus, opposite = neighbours(me)
+        return (opposite, plus, minus, me), axis_x
+
+    def across(self, h, k):
+        s, d, z, c, hi, q = self.spot
+        places, axis_x = self.lines(h)
+
+        def line(ref):
+            return ref.at[places[k], :, h] if axis_x else ref.at[:, places[k], h]
+
+        return remote(line(self.away), line(self.near), self.cs.at[h, k], self.cr.at[h, k], 2 * z + 1 - c, d)
+
+    def each(self, h, k, body):
+        places, axis_x = self.lines(h)
+
+        def one(t):
+            a, r = lax.div(t, 4), lax.rem(t, 4)
+            px, py = (places[k], a) if axis_x else (a, places[k])
+            body((px, py, h, r), jnp.minimum(4 * px + py, 14), 4 * h + r)
+
+        loop(0, 16, one)
+
+    def give(self, h, k):
         c = self.spot[3]
-        px, py = lax.div(piece, 4), lax.rem(piece, 4)
-
-        def rows(row):
-            self.away[px, py, row] = self.block(piece, row, 1 - c).astype(BF16)
-
-        loop(0, NZ, rows)
-        self.across(piece).start()
-
-    def take(self, piece):
+
+        def fill(at, piece, row):
+            self.away[at] = self.block(piece, row, 1 - c).astype(BF16)
+
+        self.each(h, k, fill)
+        self.across(h, k).start()
+
+    def take(self, h, k):
         c = self.spot[3]
-        px, py = lax.div(piece, 4), lax.rem(piece, 4)
-        self.across(piece).wait_recv()
-
-        def rows(row):
-            here = self.block(piece, row, c) + self.near[px, py, row].astype(F32)
-            self.half[px, py, lax.div(row, 4), lax.rem(row, 4)] = here.astype(BF16)
-
-        loop(0, NZ, rows)
-
-    def clear(self):
-        def rows(row):
-            self.half[3, 3, lax.div(row, 4), lax.rem(row, 4)] = jnp.zeros((ROWS, 128), BF16)
-
-        loop(0, NZ, rows)
-
-    def cut(self, h, stage, where, low, count):
+        self.across(h, k).wait_recv()
+
+        def fill(at, piece, row):
+            self.half[at] = (self.block(piece, row, c) + self.near[at].astype(F32)).astype(BF16)
+
+        self.each(h, k, fill)
+
+    def plane(self, h, stage, part, way):
+        s, d, z, c, hi, q = self.spot
+        x, y = lax.div(q, 4), lax.rem(q, 4)
+        places, axis_x = self.lines(h, stage)
+        place = places[0] if part == 0 else places[1 + way]
+        rows = pl.ds(2 * (1 - way) if part == 1 else 2 * way, 2)
+        if stage == 0:
+            piece = self.half.at[place, :, h, rows] if axis_x else self.half.at[:, place, h, rows]
+            landing = self.a1.at[h, way] if part == 0 else self.a2.at[h, way, :, rows]
+        else:
+            piece = self.half.at[place, y, h, rows] if axis_x else self.half.at[x, place, h, rows]
+            landing = self.b1.at[h, way] if part == 0 else self.b2.at[h, way, rows]
+        at = (h, 3 * stage + part, way)
+        return remote(piece, landing, self.ps.at[at], self.pr.at[at], s, plane_device(h, stage, way, hi, x, y))
+
+    def add(self, h, stage, last):
         q = self.spot[5]
         x, y = lax.div(q, 4), lax.rem(q, 4)
-        rows = pl.ds(low, count)
-        axis_x = (h == 0) == (stage == 0)
-        if stage == 0:
-            return self.half.at[where, :, h, rows] if axis_x else self.half.at[:, where, h, rows]
-        return self.half.at[where, y, h, rows] if axis_x else self.half.at[x, where, h, rows]
-
-    def plane(self, h, step, way):
-        s, d, z, c, hi, q = self.spot
-        x, y = lax.div(q, 4), lax.rem(q, 4)
-        stage, second = step // 2, step % 2
-        axis_x = (h == 0) == (stage == 0)
-        near = neighbours(x if axis_x else y)
-        if second:
-            piece = self.cut(h, stage, near[way], 0, 4)
-        else:
-            piece = self.cut(h, stage, near[2], 2 * way, 2)
-        landing = ((self.a1, self.a2), (self.b1, self.b2))[stage][second].at[h, way]
-        to = plane_device(h, stage, way, hi, x, y)
-        return remote(piece, landing, self.ps.at[h, step, way], self.pr.at[h, step, way], s, to)
-
-    def add(self, h, step):
-        q = self.spot[5]
-        x, y = lax.div(q, 4), lax.rem(q, 4)
-        stage, second = step // 2, step % 2
-        axis_x = (h == 0) == (stage == 0)
-        me = x if axis_x else y
-        near = neighbours(me)
-        landing = ((self.a1, self.a2), (self.b1, self.b2))[stage][second]
-
-        def spot_of(where, a, row):
+        places, axis_x = self.lines(h, stage)
+
+        def spot_of(place, a, row):
             if stage == 0:
-                return (where, a, h, row) if axis_x else (a, where, h, row)
-            return (where, y, h, row) if axis_x else (x, where, h, row)
+                return (place, a, h, row) if axis_x else (a, place, h, row)
+            return (place, y, h, row) if axis_x else (x, place, h, row)
 
         def one(t):
-            a, r = (lax.div(t, 4 if second else 2), lax.rem(t, 4 if second else 2))
-            if second:
-                at = spot_of(me, a, r)
+            if last:
+                a, r = lax.div(t, 4), lax.rem(t, 4)
+                at = spot_of(places[3], a, r)
                 total = self.half[at].astype(F32)
                 for way in range(2):
-                    total += (landing[h, way, a, r] if stage == 0 else landing[h, way, r]).astype(F32)
+                    total += (self.a2[h, way, a, r] if stage == 0 else self.b2[h, way, r]).astype(F32)
                 self.half[at] = total.astype(BF16)
             else:
+                a, r = lax.div(t, 2), lax.rem(t, 2)
                 for way in range(2):
-                    at = spot_of(near[way], a, 2 * way + r)
-                    here = landing[h, way, a, r] if stage == 0 else landing[h, way, r]
+                    at = spot_of(places[1 + way], a, 2 * way + r)
+                    here = self.a1[h, way, a, r] if stage == 0 else self.b1[h, way, r]
                     self.half[at] = (self.half[at].astype(F32) + here.astype(F32)).astype(BF16)
 
-        loop(0, (4 if stage == 0 else 1) * (4 if second else 2), one)
+        loop(0, (4 if stage == 0 else 1) * (4 if last else 2), one)
+
+    def begin(self, beside):
+        for k in range(4):
+            for h in range(2):
+                self.give(h, k)
+                beside()
 
     def in_four(self, i):
         s, d, z, c, hi, q = self.spot
@@ -309,25 +314,39 @@
         to = hi * NXY + lax.rem(q + i, NXY)
         return remote(self.out.at[q], self.out.at[q], self.ss.at[i - 1], self.sr.at[i - 1], s, to)
 
-    def sum_up(self, beside):
-        s, d, z, c, hi, q = self.spot
-        loop(0, 15, self.take)
-        for step in range(4):
+    def sum_up(self, beside, between):
+        s, d, z, c, hi, q = self.spot
+        ways = [(h, way) for h in range(2) for way in range(2)]
+        for stage in range(2):
+            for part in range(2):
+                for h in range(2):
+                    if stage == 0:
+                        for k in (0,) if part == 0 else (1, 2):
+                            self.take(h, k)
+                            beside()
+                    for way in range(2):
+                        self.plane(h, stage, part, way).start()
+            if stage == 0:
+                for h in range(2):
+                    self.take(h, 3)
+                    beside()
+                between()
+            beside()
             for h in range(2):
-                if step:
-                    for way in range(2):
-                        self.plane(h, step - 1, way).wait_recv()
-                    self.add(h, step - 1)
                 for way in range(2):
-                    self.plane(h, step, way).start()
-            beside(step)
-        for h in range(2):
-            for way in range(2):
-                self.plane(h, 3, way).wait_recv()
-            self.add(h, 3)
+                    self.plane(h, stage, 0, way).wait_recv()
+                self.add(h, stage, False)
+                for way in range(2):
+                    self.plane(h, stage, 2, way).start()
+            beside()
+            for h in range(2):
+                for way in range(2):
+                    for part in (1, 2):
+                        self.plane(h, stage, part, way).wait_recv()
+                self.add(h, stage, True)
         px, py, four, at = lax.div(q, 4), lax.rem(q, 4), lax.div(z, 4), lax.rem(z, 4)
         loop(1, 4, lambda i: self.in_four(i).start())
-        beside(4)
+        beside()
         loop(1, 4, lambda i: self.in_four(i).wait_recv())
         for block in range(2):
             total = self.half[px, py, block, at].astype(F32)
@@ -336,7 +355,7 @@
             self.half[px, py, block, at] = total.astype(BF16)
         for k in range(3):
             self.far_off(k).start()
-        beside(5)
+        beside()
         for k in range(3):
             self.far_off(k).wait_recv()
         total = self.half[px, py, four, at].astype(F32)
@@ -344,15 +363,17 @@
             total += self.column[k].astype(F32)
         self.out[q] = total.astype(BF16)
         loop(1, NXY, lambda i: self.spread(i).start())
-        beside(6)
+        beside()
         loop(1, NXY, lambda i: self.spread(i).wait())
 
     def finish(self):
-        loop(0, 15, lambda piece: self.across(piece).wait_send())
         for h in range(2):
-            for step in range(4):
-                for way in range(2):
-                    self.plane(h, step, way).wait_send()
+            for k in range(4):
+                self.across(h, k).wait_send()
+            for stage in range(2):
+                for part in range(3):
+                    for way in range(2):
+                        self.plane(h, stage, part, way).wait_send()
         loop(1, 4, lambda i: self.in_four(i).wait_send())
         for k in range(3):
             self.far_off(k).wait_send()
@@ -451,16 +472,17 @@
     away[ch, frames] = (rate * (grad - mean - unit * along)).reshape(GROUP, CP, D).astype(BF16)
 
 
-def weight_partial(first, count, i, normed, gproj, gw):
+def weight_partial(first, count, normed, gproj, gw):
     rows = pl.ds(first * TOK, count * TOK)
 
     def part(n):
         cut = pl.ds(pl.multiple_of(n * 384, 128), 384)
-        term = dot_first(normed[rows, cut], gproj[i, rows, :])
-        if first == 0:
-            gw[i, cut, :] = term
-        else:
-            gw[i, cut, :] += term
+        for i in range(3):
+            term = dot_first(normed[rows, cut], gproj[i, rows, :])
+            if first == 0:
+                gw[i, cut, :] = term
+            else:
+                gw[i, cut, :] += term
 
     loop(0, 3, part)
 
@@ -566,7 +588,6 @@
             column_of = lax.broadcasted_iota(jnp.int32, (2 * TOK, TOK), 1)
             block[...] = jnp.where(lax.rem(row, CP) == lax.rem(column_of, CP), 0.0, -1e30)
             cot[:, pl.ds(512, 128)] = jnp.zeros((TOK, 128), BF16)
-            total.clear()
             for keep in keeps:
                 keep.wait()
 
@@ -589,33 +610,39 @@
 
     def early(ch):
         forward(ch)
-        backward(ch)
-        keep_back(ch).start()
+
+        @pl.when(ch < 2)
+        def _():
+            backward(ch)
+            keep_back(ch).start()
 
         @pl.when(ch == 1)
         def _():
-            loop(0, 3, lambda i: weight_partial(0, 2, i, normed, gproj, gw))
+            weight_partial(0, 2, normed, gproj, gw)
 
     loop(0, 3, early)
-    loop(0, 3, lambda i: weight_partial(2, 1, i, normed, gproj, gw))
+    weight_partial(2, 1, normed, gproj, gw)
     sent_all(send_x, 3)
-    give_back(0, RETURNS[0])
+    counts, started = iter(RETURNS), [0]
+
+    def beside():
+        first = started[0]
+        started[0] = min(first + next(counts), 60)
+        give_back(first, started[0])
+
+    beside()
     forward(3)
-
-    def part(i):
-        weight_partial(3, 1, i, normed, gproj, gw)
-        loop(0, 5, lambda t: total.give(5 * i + t))
-
-    loop(0, 3, part)
-    give_back(RETURNS[0], RETURNS[1])
-
-    def beside(step):
-        if step == 0:
-            backward(3)
-            keep_back(3).start()
-        give_back(RETURNS[step + 1], RETURNS[step + 2])
-
-    total.sum_up(beside)
+    beside()
+    weight_partial(3, 1, normed, gproj, gw)
+    beside()
+    total.begin(beside)
+
+    def last_chunk():
+        for ch in (2, 3):
+            backward(ch)
+            keep_back(ch).start()
+
+    total.sum_up(beside, last_chunk)
     gout[...] = narrow([jnp.concatenate([tiles[5 * i + t].astype(F32) for t in range(5)], axis=1) for i in range(3)]).astype(
         BF16
     )
@@ -633,8 +660,8 @@
     loop(0, CH, finish)
 
 
-FEEDS = (0, 6, 11, 16, 20, 30, 36, 40)
-RETURNS = (10, 20, 25, 34, 39, 43, 47, 51, 60)
+FEEDS = (0, 8, 14, 20, 26, 38, 46, 52)
+RETURNS = (10, 6, 6) + (0,) * 16 + (4, 5, 3, 3, 4, 4, 60)
 
 
 def fused(x, cot, shift, scale, w):
@@ -665,8 +692,8 @@
             pltpu.VMEM((2, 4, ROWS, 128), BF16),
             pltpu.VMEM((4, 4, 2, 4, ROWS, 128), BF16),
             pltpu.VMEM((4, 4, 2, 4, ROWS, 128), BF16),
-            pltpu.VMEM((4, 4, NZ, ROWS, 128), BF16),
-            pltpu.VMEM((4, 4, NZ, ROWS, 128), BF16),
+            pltpu.VMEM((4, 4, 2, 4, ROWS, 128), BF16),
+            pltpu.VMEM((4, 4, 2, 4, ROWS, 128), BF16),
             pltpu.VMEM((4, 4, 2, 4, ROWS, 128), BF16),
             pltpu.VMEM((2, 2, 4, 2, ROWS, 128), BF16),
             pltpu.VMEM((2, 2, 4, 4, ROWS, 128), BF16),
@@ -686,10 +713,10 @@
             dma((2, 4, 2)),
             dma((2, 7)),
             dma((2, 7)),
-            dma((15,)),
-            dma((15,)),
-            dma((2, 4, 2)),
-            dma((2, 4, 2)),
+            dma((2, 4)),
+            dma((2, 4)),
+            dma((2, 6, 2)),
+            dma((2, 6, 2)),
             dma((6,)),
             dma((6,)),
             dma((NXY - 1,)),

time: 175 us -> 169 us (0.966)
  Pallas kernels: 171 us -> 165 us
    pallas_call x1, Pallas kernels: 171 us -> 165 us  [fused(): pl.pallas_call(kernel, out_shape=(jax.ShapeDtypeStruct(x.shape, BF16), ja...]
where the time goes in v5:
time: 169 us; the launch traced here: 168 us
  Pallas kernels  165 us (98%)
  local copies, waits for them, and re-layouts  3.12 us (2%)
    pallas_call x1, Pallas kernels, fused(): pl.pallas_call(kernel, out_shape=(jax.ShapeDtypeStruct(x.shape, BF16), ja...  165 us

profile of v5, /device:TPU:1, one launch (start us, length us, event | category | flops | bytes accessed | tf_op | source)
XLA Modules:
  0.0 168.4 jit_solution(2768419268769042937)
XLA Ops:
  0.6 164.6 %temporal_backward.1 = (bf16[64,8,1152]{2,1,0:T(8,128)(2,1)}, bf16[72,1728]{1,0:T(8,128)(2,1)}) custom-call(bf16[64,8,1152]{2,1,0:T(8,128)(2,1)} %bitcast.5, bf16[576,512]{1,0:T(8,128)(2,1)} %bitcast.7, f32[1,1152]{1,0:T(1,128)} %shift.1, f32[1,1152]{1,0:T(1,128)} %scale.1, bf16[72,1728]{1,0:T(8,128)(2,1)} %w_in.1), custom_call_target="tpu_custom_call" | custom-call | tf_op jit(solution)/shard_map/temporal_backward/pallas_call | solution.py:670
  165.3 0.0 copy-start
  165.3 2.4 %copy.9 = bf16[1,1,512,1152]{3,2,1,0:T(8,128)(2,1)} copy(bf16[1,1,512,1152]{3,2,1,0:T(8,128)(2,1)} %bitcast.6) | data formatting | bytes 2359296
  167.7 0.0 copy-done
  167.7 0.7 copy.10
Async XLA Ops:
  165.3 2.4 %copy-start = (bf16[72,1728]{1,0:T(8,128)(2,1)S(1)}, bf16[72,1728]{1,0:T(8,128)(2,1)}, u32[]{:S(2)}) copy-start(bf16[72,1728]{1,0:T(8,128)(2,1)} %get-tuple-element.9) | copy-start | bytes 746500

commit v6 on v5

--- a/solution.py
+++ b/solution.py
@@ -49,6 +49,10 @@
         return carry
 
     lax.fori_loop(start, stop, step, 0)
+
+
+def wrap(place):
+    return jnp.where(place >= 16, place - 16, place)
 
 
 def greet(seq, dp):
@@ -179,8 +183,8 @@
         loop(0, 15 * NZ, assemble)
 
     def finish(self):
-        self.along_z(0).wait_send()
-        loop(1, 4, lambda i: self.along_z(i).wait_send())
+        for i in range(4):
+            self.along_z(i).wait_send()
         self.own_across().wait_send()
         for h in range(2):
             for step in range(4):
@@ -311,10 +315,10 @@
 
     def spread(self, i):
         s, d, z, c, hi, q = self.spot
-        to = hi * NXY + lax.rem(q + i, NXY)
+        to = hi * NXY + wrap(q + i)
         return remote(self.out.at[q], self.out.at[q], self.ss.at[i - 1], self.sr.at[i - 1], s, to)
 
-    def sum_up(self, beside, between):
+    def sum_up(self, beside, between, settle):
         s, d, z, c, hi, q = self.spot
         ways = [(h, way) for h in range(2) for way in range(2)]
         for stage in range(2):
@@ -362,9 +366,12 @@
         for k in range(3):
             total += self.column[k].astype(F32)
         self.out[q] = total.astype(BF16)
-        loop(1, NXY, lambda i: self.spread(i).start())
+        for i in range(1, NXY):
+            self.spread(i).start()
         beside()
-        loop(1, NXY, lambda i: self.spread(i).wait())
+        settle()
+        for i in range(1, NXY):
+            self.spread(i).wait()
 
     def finish(self):
         for h in range(2):
@@ -504,8 +511,10 @@
     total = Reduce(
         (gw, tiles, far, near, half, a1, a2, b1, b2, fours, column, rcs, rcr, rps, rpr, rzs, rzr, rss, rsr), spot
     )
-    loop(1, SEQ, lambda i: greet(lax.rem(s + i, SEQ), d))
-    loop(1, NXY, lambda i: greet(s, hi * NXY + lax.rem(q + i, NXY)))
+    for i in range(1, SEQ):
+        greet(wrap(s + i), d)
+    for i in range(1, NXY):
+        greet(s, hi * NXY + wrap(q + i))
     for at in (z, lax.rem(z + 4, NZ)):
         greet(2 * at + c, (1 - hi) * NXY + q)
 
@@ -513,25 +522,27 @@
         return j * CH + ch
 
     def send_x(ch, i):
-        j = lax.rem(s + i, SEQ)
+        j = wrap(s + i)
         return remote(x.at[group_of(j, ch)], tokens.at[ch, s], sx.at[ch, i - 1], rx.at[ch, i - 1], j, d)
 
     def send_c(pair, i):
-        j = lax.rem(s + i, SEQ)
+        j = wrap(s + i)
         return remote(paired.at[j, pair], cots.at[pair, s], sc.at[pair, i - 1], rc.at[pair, i - 1], j, d)
 
     def send_back(ch, i):
-        j = lax.rem(s + i, SEQ)
+        j = wrap(s + i)
         return remote(away.at[ch, j], out.at[group_of(s, ch)], sb.at[ch, i - 1], rb.at[ch, i - 1], j, d)
 
     def keep_back(ch):
         return pltpu.make_async_copy(away.at[ch, s], out.at[group_of(s, ch)], own_sems.at[1 + ch])
 
     def sent_all(copy, k):
-        loop(1, SEQ, lambda i: copy(k, i).wait_send())
+        for i in range(1, SEQ):
+            copy(k, i).wait_send()
 
     def came_all(copy, k):
-        loop(1, SEQ, lambda i: copy(k, i).wait_recv())
+        for i in range(1, SEQ):
+            copy(k, i).wait_recv()
 
     order = ((send_x, 0), (send_c, 0), (send_x, 1), (send_x, 2), (send_c, 1), (send_x, 3))
 
@@ -539,10 +550,12 @@
         for k, (copy, which) in enumerate(order):
             low, high = max(first - 15 * k, 0), min(last - 15 * k, 15)
             if low < high:
-                loop(low + 1, high + 1, lambda i: copy(which, i).start())
+                for i in range(low + 1, high + 1):
+                    copy(which, 7 * i % SEQ).start()
 
     def give_back(first, last):
-        loop(first, last, lambda n: send_back(lax.div(n, 15), lax.rem(n, 15) + 1).start())
+        for n in range(first, last):
+            send_back(n // 15, n % 15 + 1).start()
 
     load = pltpu.make_async_copy(w_in, rows_in, own_sems.at[0])
     turn = pltpu.make_async_copy(cot_in, turned, own_sems.at[1 + CH])
@@ -642,26 +655,30 @@
             backward(ch)
             keep_back(ch).start()
 
-    total.sum_up(beside, last_chunk)
+    def returned(ch):
+        for i in range(1, SEQ):
+            send_back(ch, i).wait()
+        keep_back(ch).wait()
+
+    def settle():
+        weight.finish()
+        for pair in range(CH // 2):
+            sent_all(send_c, pair)
+        for ch in range(CH - 1):
+            sent_all(send_x, ch)
+        total.finish()
+        for ch in range(CH - 1):
+            returned(ch)
+
+    total.sum_up(beside, last_chunk, settle)
     gout[...] = narrow([jnp.concatenate([tiles[5 * i + t].astype(F32) for t in range(5)], axis=1) for i in range(3)]).astype(
         BF16
     )
-    total.finish()
-    weight.finish()
-    for pair in range(CH // 2):
-        sent_all(send_c, pair)
-    for ch in range(3):
-        sent_all(send_x, ch)
-
-    def finish(ch):
-        loop(1, SEQ, lambda i: send_back(ch, i).wait())
-        keep_back(ch).wait()
-
-    loop(0, CH, finish)
+    returned(CH - 1)
 
 
 FEEDS = (0, 8, 14, 20, 26, 38, 46, 52)
-RETURNS = (10, 6, 6) + (0,) * 16 + (4, 5, 3, 3, 4, 4, 60)
+RETURNS = (10, 6, 6) + (0,) * 16 + (6, 6, 3, 2, 3, 3, 60)
 
 
 def fused(x, cot, shift, scale, w):

time: 169 us -> 167 us (0.988)
  Pallas kernels: 165 us -> 163 us
where the time goes in v6:
time: 167 us
  Pallas kernels  163 us (98%)
  local copies, waits for them, and re-layouts  3.12 us (2%)
    pallas_call x1, Pallas kernels, fused(): pl.pallas_call(kernel, out_shape=(jax.ShapeDtypeStruct(x.shape, BF16), ja...  163 us

profile of v6, /device:TPU:1, one launch (start us, length us, event | category | flops | bytes accessed | tf_op | source)
XLA Modules:
  0.0 166.7 jit_solution(2617383254794221809)
XLA Ops:
  0.6 163.0 %temporal_backward.1 = (bf16[64,8,1152]{2,1,0:T(8,128)(2,1)}, bf16[72,1728]{1,0:T(8,128)(2,1)}) custom-call(bf16[64,8,1152]{2,1,0:T(8,128)(2,1)} %bitcast.5, bf16[576,512]{1,0:T(8,128)(2,1)} %bitcast.7, f32[1,1152]{1,0:T(1,128)} %shift.1, f32[1,1152]{1,0:T(1,128)} %scale.1, bf16[72,1728]{1,0:T(8,128)(2,1)} %w_in.1), custom_call_target="tpu_custom_call" | custom-call | tf_op jit(solution)/shard_map/temporal_backward/pallas_call | solution.py:687
  163.6 0.0 copy-start
  163.6 2.4 %copy.9 = bf16[1,1,512,1152]{3,2,1,0:T(8,128)(2,1)} copy(bf16[1,1,512,1152]{3,2,1,0:T(8,128)(2,1)} %bitcast.6) | data formatting | bytes 2359296
  166.0 0.0 copy-done
  166.0 0.7 copy.10
Async XLA Ops:
  163.6 2.4 %copy-start = (bf16[72,1728]{1,0:T(8,128)(2,1)S(1)}, bf16[72,1728]{1,0:T(8,128)(2,1)}, u32[]{:S(2)}) copy-start(bf16[72,1728]{1,0:T(8,128)(2,1)} %get-tuple-element.9) | copy-start | bytes 746500

commit v7 on v6

--- a/solution.py
+++ b/solution.py
@@ -688,7 +688,7 @@
         kernel,
         out_shape=(jax.ShapeDtypeStruct(x.shape, BF16), jax.ShapeDtypeStruct((ROWS, 3 * INNER), BF16)),
         in_specs=[hbm, hbm, vm, vm, hbm],
-        out_specs=(vm, vm),
+        out_specs=(hbm, vm),
         scratch_shapes=[
             pltpu.VMEM((ROWS, 3 * INNER), BF16),
             pltpu.VMEM((INNER, PATCH), BF16),

time: 167 us -> 167 us (level)
  no operation moved by 1% of the time
where the time goes in v7:
time: 167 us; the launch traced here: 166 us
  Pallas kernels  163 us (98%)
  local copies, waits for them, and re-layouts  3.12 us (2%)
    pallas_call x1, Pallas kernels, fused(): pl.pallas_call(kernel, out_shape=(jax.ShapeDtypeStruct(x.shape, BF16), ja...  163 us

profile of v7, /device:TPU:1, one launch (start us, length us, event | category | flops | bytes accessed | tf_op | source)
XLA Modules:
  0.0 166.4 jit_solution(2185396184505273800)
XLA Ops:
  0.6 162.6 %temporal_backward.1 = (bf16[64,8,1152]{2,1,0:T(8,128)(2,1)}, bf16[72,1728]{1,0:T(8,128)(2,1)}) custom-call(bf16[64,8,1152]{2,1,0:T(8,128)(2,1)} %bitcast.5, bf16[576,512]{1,0:T(8,128)(2,1)} %bitcast.7, f32[1,1152]{1,0:T(1,128)} %shift.1, f32[1,1152]{1,0:T(1,128)} %scale.1, bf16[72,1728]{1,0:T(8,128)(2,1)} %w_in.1), custom_call_target="tpu_custom_call" | custom-call | tf_op jit(solution)/shard_map/temporal_backward/pallas_call | solution.py:687
  163.3 0.0 copy-start
  163.3 2.4 %copy.9 = bf16[1,1,512,1152]{3,2,1,0:T(8,128)(2,1)} copy(bf16[1,1,512,1152]{3,2,1,0:T(8,128)(2,1)} %bitcast.6) | data formatting | bytes 2359296
  165.7 0.0 copy-done
  165.7 0.7 copy.10
Async XLA Ops:
  163.3 2.4 %copy-start = (bf16[72,1728]{1,0:T(8,128)(2,1)S(1)}, bf16[72,1728]{1,0:T(8,128)(2,1)}, u32[]{:S(2)}) copy-start(bf16[72,1728]{1,0:T(8,128)(2,1)} %get-tuple-element.9) | copy-start | bytes 746500
